TPU v7x, 32 devices: a whole 2x2x4 slice. The times are simulated.
32 devices in a mesh: seq: 8 (over z, x), head: 4 (over y, core).
Axes of the slice: x: 2, y: 2, z: 4, core: 2. Of those that a mesh axis runs over, the one named last changes fastest.
Arguments:
- queries: bfloat16 [8192, 2048], P('seq', 'head'), may hold values from -108 to 108
- pool: bfloat16 [256, 128, 896], P('seq', 'head'), may hold values from -6 to 6
- w_key: bfloat16 [896, 2048], P(None, 'head'), may hold values from -0.1875 to 0.1875
- w_value: bfloat16 [896, 2048], P(None, 'head'), may hold values from -0.1875 to 0.1875
- out_grad: bfloat16 [8192, 2048], P('seq', 'head'), may hold values from -1.5 to 1.5
- nb_source: int32 [128, 2], replicated, may hold values from 0 to 7, all different within a row; in each aligned block of 16 rows (0 to 15, 16 to 31, ...) at most 8 rows name the same one
- nb_slot: int32 [128, 2], replicated, may hold values from 0 to 31
- nb_count: int32 [128], replicated, may hold values from 1 to 2
Outputs:
- attended: bfloat16 [8192, 2048], P('seq', 'head')
- grad_queries: bfloat16 [8192, 2048], P('seq', 'head')
- grad_pool: float32 [256, 128, 896], P('seq', 'head')
- grad_w_key: float32 [896, 2048], P(None, 'head')
- grad_w_value: float32 [896, 2048], P(None, 'head')
Inputs may be any that keep to these rules, and one draw needn't show every extreme that they name: `nb_source`: for the 16 stretches of one device (aligned blocks of stretches), no encoder device is named by more than 8 entries, and in some block one is named exactly 8 times; the 2 neighbours of a stretch come from different encoder devices.
All inputs are finite; a program needn't handle non-finite values.
Results may differ from a plain program's by a relative error of at most 0.018.
The roundings to bfloat16 on the way count: a program that leaves them out, or rounds other values in their place, can miss the bound.
Values may be sent and summed in bfloat16 or wider, within the bound.
A program may use at most 128 MiB of HBM per device.

v0:
```python
import math

import jax
import jax.numpy as jnp
from jax import lax
from jax.sharding import PartitionSpec as P

DH = 128
STRETCH = 64
KNB = 2
CH_DEV = 16


def local(queries, pool, w_key, w_value, out_grad, nb_source, nb_slot, nb_count):
    f32 = jnp.float32
    seq_count = lax.axis_size("seq")
    seq_index = lax.axis_index("seq")
    requests = CH_DEV * KNB
    capacity = max(2, 2 * requests // seq_count)
    slot_span = seq_count * capacity
    source_table = nb_source.reshape(seq_count, requests)
    slot_table = nb_slot.reshape(seq_count, requests)
    order_ids = jnp.arange(requests)
    matches = source_table[:, :, None] == source_table[:, None, :]
    before = order_ids[None, :] < order_ids[:, None]
    ranks = jnp.sum(jnp.logical_and(matches, before[None, :, :]), axis=2)
    places = jnp.arange(capacity)
    chosen = jnp.logical_and(
        (source_table == seq_index)[:, :, None], ranks[:, :, None] == places[None, None, :]
    )
    picked_slot = jnp.sum(jnp.where(chosen, slot_table[:, :, None], 0), axis=1).reshape(slot_span)
    filled = jnp.any(chosen, axis=1).reshape(slot_span)
    outgoing = jnp.take(pool, picked_slot, axis=0)
    outgoing = jnp.where(filled[:, None, None], outgoing, jnp.zeros_like(outgoing))
    incoming = lax.all_to_all(outgoing, "seq", split_axis=0, concat_axis=0, tiled=True)
    own_sources = lax.dynamic_index_in_dim(source_table, seq_index, 0, keepdims=False)
    own_ranks = lax.dynamic_index_in_dim(ranks, seq_index, 0, keepdims=False)
    positions = own_sources * capacity + own_ranks
    enc_width = pool.shape[2]
    local_width = w_key.shape[1]
    head_count = local_width // DH
    both_weights = jnp.concatenate([w_key, w_value], axis=1)
    wanted = jnp.take(incoming, positions, axis=0)
    panel_piece = lax.all_gather(wanted, "head", axis=1, tiled=True)
    projected = jnp.einsum(
        "jre,ec->jrc", panel_piece, both_weights, preferred_element_type=f32
    ).astype(jnp.bfloat16)
    joined = jnp.concatenate([panel_piece, projected], axis=2)
    panels = joined[:, :, :enc_width]
    rows_full = joined.shape[1]
    keys = joined[:, :, enc_width : enc_width + local_width].reshape(
        CH_DEV, KNB, rows_full, head_count, DH
    )
    values = joined[:, :, enc_width + local_width :].reshape(CH_DEV, KNB, rows_full, head_count, DH)
    query_blocks = queries.reshape(CH_DEV, STRETCH, head_count, DH)
    grad_blocks = out_grad.reshape(CH_DEV, STRETCH, head_count, DH)
    used_counts = lax.dynamic_slice_in_dim(nb_count, seq_index * CH_DEV, CH_DEV)
    used_mask = (jnp.arange(KNB)[None, :] < used_counts[:, None])[:, None, None, :, None]
    factor = 1.0 / math.sqrt(DH)
    scores = (
        jnp.einsum("cqhd,ckrhd->chqkr", query_blocks, keys, preferred_element_type=f32) * factor
    )
    masked_scores = jnp.where(used_mask, scores, -jnp.inf)
    row_max = jnp.max(masked_scores, axis=(3, 4), keepdims=True)
    exp_scores = jnp.where(used_mask, jnp.exp(masked_scores - row_max), 0.0)
    soft_probs = exp_scores / jnp.sum(exp_scores, axis=(3, 4), keepdims=True)
    soft_weights = soft_probs.astype(jnp.bfloat16)
    attended = jnp.einsum(
        "chqkr,ckrhd->cqhd", soft_weights, values, preferred_element_type=f32
    ).astype(jnp.bfloat16)
    grad_probs = jnp.einsum("cqhd,ckrhd->chqkr", grad_blocks, values, preferred_element_type=f32)
    row_dot = jnp.sum(soft_probs * grad_probs, axis=(3, 4), keepdims=True)
    grad_scores = (soft_probs * (grad_probs - row_dot)).astype(jnp.bfloat16)
    grad_queries = (
        jnp.einsum("chqkr,ckrhd->cqhd", grad_scores, keys, preferred_element_type=f32) * factor
    ).astype(jnp.bfloat16)
    grad_keys = (
        jnp.einsum("chqkr,cqhd->ckrhd", grad_scores, query_blocks, preferred_element_type=f32)
        * factor
    ).astype(jnp.bfloat16)
    grad_values = jnp.einsum(
        "chqkr,cqhd->ckrhd", soft_weights, grad_blocks, preferred_element_type=f32
    ).astype(jnp.bfloat16)
    grad_keys = grad_keys.reshape(requests, rows_full, local_width)
    grad_values = grad_values.reshape(requests, rows_full, local_width)
    summed = lax.psum_scatter(
        (
            jnp.einsum("jrc,ec->rje", grad_keys, w_key, preferred_element_type=f32)
            + jnp.einsum("jrc,ec->rje", grad_values, w_value, preferred_element_type=f32)
        ).astype(jnp.bfloat16),
        "head",
        scatter_dimension=0,
        tiled=True,
    )
    spread = (positions[None, :] == jnp.arange(slot_span)[:, None]).astype(jnp.bfloat16)
    returning = jnp.einsum("qj,rje->rqe", spread, summed, preferred_element_type=f32).astype(
        jnp.bfloat16
    )
    arrived = lax.all_to_all(returning, "seq", split_axis=1, concat_axis=1, tiled=True)
    pool_count = pool.shape[0]
    collect = jnp.logical_and(
        picked_slot[None, :] == jnp.arange(pool_count)[:, None], filled[None, :]
    ).astype(jnp.bfloat16)
    grad_pool = jnp.einsum("pq,rqe->pre", collect, arrived, preferred_element_type=f32)
    key_partial = jnp.einsum("jre,jrc->ec", panels, grad_keys, preferred_element_type=f32)
    value_partial = jnp.einsum("jre,jrc->ec", panels, grad_values, preferred_element_type=f32)
    grad_w_key, grad_w_value = lax.psum((key_partial, value_partial), "seq")
    token_rows = queries.shape[0]
    return (
        attended.reshape(token_rows, local_width),
        grad_queries.reshape(token_rows, local_width),
        grad_pool,
        grad_w_key,
        grad_w_value,
    )


def solution(mesh):
    return jax.shard_map(
        local,
        mesh=mesh,
        in_specs=(
            P("seq", "head"),
            P("seq", "head", None),
            P(None, "head"),
            P(None, "head"),
            P("seq", "head"),
            P(),
            P(),
            P(),
        ),
        out_specs=(
            P("seq", "head"),
            P("seq", "head"),
            P("seq", "head", None),
            P(None, "head"),
            P(None, "head"),
        ),
        check_vma=False,
    )
```

profile of v0, /device:TPU:8, one launch (start us, length us, event | category | flops | bytes accessed | tf_op | source)
XLA Modules:
  0.0 522.0 jit_solution(16944285833424488035)
XLA Ops:
  10.1 2.8 gather_fusion
  12.9 4.5 select_select_fusion
  17.4 6.3 %all-to-all-start = ((bf16[64,32,896]{2,1,0:T(8,128)(2,1)}), bf16[64,32,896]{2,1,0:T(8,128)(2,1)}, u32[]{:S(2)}, u32[]{:S(2)}) async-start(bf16[64,32,896]{2,1,0:T(8,128)(2,1)} %select_select_fusion), calls=%async_computation | async-start | bytes 7340032 | tf_op jit(solution)/shard_map/all_to_all | solution.py:35
  23.7 79.4 %all-to-all-done = bf16[64,32,896]{2,1,0:T(8,128)(2,1)} async-done(((bf16[64,32,896]{2,1,0:T(8,128)(2,1)}), bf16[64,32,896]{2,1,0:T(8,128)(2,1)}, u32[]{:S(2)}, u32[]{:S(2)}) %all-to-all-start) | async-done | bytes 3670048 | tf_op jit(solution)/shard_map/all_to_all | solution.py:35
  103.2 2.9 gather_fusion.1
  106.1 1.5 broadcast_select_fusion
  108.1 1.3 reshape.173
  109.6 51.6 %all-gather.2.cloned.1.call-done = bf16[32,128,896]{2,1,0:T(8,128)(2,1)} async-done(((bf16[32,32,896]{2,1,0:T(8,128)(2,1)}), bf16[32,128,896]{2,1,0:T(8,128)(2,1)}) %all-gather.2.cloned.1.call-update) | async-done | bytes 7340048 | tf_op jit(solution)/shard_map/all_gather | solution.py:44
  161.2 11.7 %convolution_convert_fusion = bf16[32,128,1024]{2,1,0:T(8,128)(2,1)S(1)} fusion(bf16[32,128,896]{2,1,0:T(8,128)(2,1)} %all-gather.2.cloned.1.call-done, bf16[896,512]{1,0:T(8,128)(2,1)} %param.11, bf16[896,512]{1,0:T(8,128)(2,1)} %param.10), kind=kOutput, calls=%fused_computation.4 | convolution fusion | flops 7524057088 | bytes 17563648 | tf_op jit(solution)/shard_map/jre,ec->jrc/dot_general | solution.py:45
  172.8 3.9 fusion.57
  176.8 6.9 %reshape.170 = bf16[16,2,128,4,128]{4,3,2,1,0:T(4,128)(2,1)} reshape(bf16[32,128,512]{2,1,0:T(8,128)(2,1)} %get-tuple-element.29) | data formatting | bytes 8388608 | tf_op jit(solution)/shard_map/reshape | solution.py:51
  183.7 6.9 %reshape.169 = bf16[16,2,128,4,128]{4,3,2,1,0:T(4,128)(2,1)} reshape(bf16[32,128,512]{2,1,0:T(8,128)(2,1)} %get-tuple-element.30) | data formatting | bytes 8388608 | tf_op jit(solution)/shard_map/reshape | solution.py:54
  190.6 3.9 bitcast_reduce_fusion
  194.5 1.7 fusion.18
  196.2 3.3 convert_bitcast_fusion
  199.5 3.5 fusion.2
  203.3 2.1 fusion.4
  208.0 8.0 %fusion.40 = f32[32,128,896]{2,1,0:T(8,128)} fusion(bf16[32,128,512]{1,2,0:T(8,128)(2,1)S(1)} %bitcast.108, bf16[896,512]{1,0:T(8,128)(2,1)S(1)} %copy-done.12), kind=kOutput, calls=%fused_computation.53 | convolution fusion | flops 3758096384 | bytes 19791872 | tf_op jit(solution)/shard_map/jrc,ec->rje/dot_general | solution.py:88
  216.0 9.8 %fusion = bf16[128,32,896]{2,0,1:T(8,128)(2,1)} fusion(f32[32,128,896]{2,1,0:T(8,128)} %fusion.40, bf16[32,128,512]{1,2,0:T(8,128)(2,1)S(1)} %bitcast.106, bf16[896,512]{1,0:T(8,128)(2,1)S(1)} %copy-done.13), kind=kOutput, calls=%fused_computation.5 | convolution fusion | flops 3765436416 | bytes 27131904 | tf_op jit(solution)/shard_map/jrc,ec->rje/dot_general | solution.py:89
  225.8 65.5 %reduce-scatter.2.cloned.1.call-done = bf16[32,32,896]{2,0,1:T(8,128)(2,1)} async-done(((bf16[128,32,896]{2,0,1:T(8,128)(2,1)}), bf16[32,32,896]{2,0,1:T(8,128)(2,1)}) %reduce-scatter.2.cloned.1.call-update) | async-done | bytes 1835024 | tf_op jit(solution)/shard_map/reduce_scatter | solution.py:86
  291.3 2.7 convert_bitcast_fusion.1
  294.1 3.9 copy.78
  298.0 6.0 %all-to-all-start.1 = ((bf16[32,64,896]{2,0,1:T(8,128)(2,1)}), bf16[32,64,896]{2,0,1:T(8,128)(2,1)}, u32[]{:S(2)}, u32[]{:S(2)}) async-start(bf16[32,64,896]{2,0,1:T(8,128)(2,1)} %copy.78), calls=%async_computation.2 | async-start | bytes 7340032 | tf_op jit(solution)/shard_map/all_to_all | solution.py:99
  304.1 9.7 %convolution_bitcast_fusion.1 = f32[896,512]{1,0:T(8,128)} fusion(bf16[32,128,896]{2,1,0:T(8,128)(2,1)} %all-gather.2.cloned.1.call-done, bf16[32,128,512]{1,2,0:T(8,128)(2,1)} %bitcast.109), kind=kOutput, calls=%fused_computation.41 | convolution fusion | flops 3758096384 | bytes 13369344 | tf_op jit(solution)/shard_map/jre,jrc->ec/dot_general | solution.py:105
  313.7 7.8 %convolution_bitcast_fusion = f32[896,512]{1,0:T(8,128)} fusion(bf16[32,128,896]{2,1,0:T(8,128)(2,1)} %all-gather.2.cloned.1.call-done, bf16[32,128,512]{1,2,0:T(8,128)(2,1)S(1)} %bitcast.107), kind=kOutput, calls=%fused_computation.40 | convolution fusion | flops 3758096384 | bytes 13369344 | tf_op jit(solution)/shard_map/jre,jrc->ec/dot_general | solution.py:106
  321.6 5.5 %fusion.27 = bf16[16,64,4,128]{3,1,2,0:T(8,128)(2,1)S(1)} fusion(bf16[16,2,128,4,128]{4,3,2,1,0:T(4,128)(2,1)} %reshape.169, f32[16,4,2,128,64]{3,4,2,1,0:T(8,128)} %copy-done.2, f32[16,4,64]{2,1,0:T(4,128)S(1)} %fusion.18, f32[16,4,64]{2,1,0:T(4,128)S(1)} %get-tuple-element.31, pred[16,2]{1,0:T(8,128)(4,1)S(1)} %iota_compare_fusion.4), kind=kOutput, calls=%fused_computation.42 | convolution fusion | flops 275251200 | bytes 9469984 | tf_op jit(solution)/shard_map/chqkr,ckrhd->cqhd/dot_general | solution.py:68
  329.6 1.7 copy_bitcast_fusion
  331.4 91.7 %all-to-all-done.1 = bf16[32,64,896]{2,0,1:T(8,128)(2,1)} async-done(((bf16[32,64,896]{2,0,1:T(8,128)(2,1)}), bf16[32,64,896]{2,0,1:T(8,128)(2,1)}, u32[]{:S(2)}, u32[]{:S(2)}) %all-to-all-start.1) | async-done | bytes 3670048 | tf_op jit(solution)/shard_map/all_to_all | solution.py:99
  423.1 4.3 fusion.15
  427.5 4.0 copy.82
  431.4 79.4 %all-reduce.3.cloned.1.call-done = (f32[896,512]{1,0:T(8,128)}, f32[896,512]{1,0:T(8,128)}) async-done(((f32[896,512]{1,0:T(8,128)}, f32[896,512]{1,0:T(8,128)}), (f32[896,512]{1,0:T(8,128)}, f32[896,512]{1,0:T(8,128)})) %all-reduce.3.cloned.1.call-update) | async-done | bytes 3670032 | tf_op jit(solution)/shard_map/psum | solution.py:107
  510.8 3.0 copy.143
  (64 shorter events, 10.2 us)
Async XLA Ops:
  7.2 3.0 copy-start
  17.4 85.7 %all-to-all-start = ((bf16[64,32,896]{2,1,0:T(8,128)(2,1)}), bf16[64,32,896]{2,1,0:T(8,128)(2,1)}, u32[]{:S(2)}, u32[]{:S(2)}) async-start(bf16[64,32,896]{2,1,0:T(8,128)(2,1)} %select_select_fusion), calls=%async_computation | async-start | bytes 7340032 | tf_op jit(solution)/shard_map/all_to_all | solution.py:35
  23.7 137.5 %all-gather.2.cloned.1.call-start = ((), (), s32[]{:S(2)}) async-start(), calls=%async_computation.3 | async-start | bytes 9175040 | tf_op jit(solution)/shard_map/all_gather | solution.py:44
  23.7 84.1 %copy-start.11 = (bf16[1024,512]{1,0:T(8,128)(2,1)S(1)}, bf16[1024,512]{1,0:T(8,128)(2,1)}, u32[]{:S(2)}) copy-start(bf16[1024,512]{1,0:T(8,128)(2,1)} %param.8) | copy-start | bytes 3145732
  106.0 3.4 copy-start.14
  107.6 183.8 %reduce-scatter.2.cloned.1.call-start = ((), (), s32[]{:S(2)}) async-start(), calls=%async_computation.4 | async-start | bytes 9175040 | tf_op jit(solution)/shard_map/reduce_scatter | solution.py:86
  194.5 8.8 %copy-start.2 = (f32[16,4,2,128,64]{3,4,2,1,0:T(8,128)}, f32[16,4,2,128,64]{3,4,2,1,0:T(8,128)S(1)}, u32[]{:S(2)}) copy-start(f32[16,4,2,128,64]{3,4,2,1,0:T(8,128)S(1)} %get-tuple-element.32) | copy-start | bytes 12582916
  196.2 3.3 copy-start.6
  203.3 12.7 %copy-start.7 = (bf16[16,2,128,4,128]{2,4,3,1,0:T(8,128)(2,1)}, bf16[16,2,128,4,128]{2,4,3,1,0:T(8,128)(2,1)S(1)}, u32[]{:S(2)}) copy-start(bf16[16,2,128,4,128]{2,4,3,1,0:T(8,128)(2,1)S(1)} %copy.75) | copy-start | bytes 12582916
  205.4 1.9 copy-start.3
  206.8 1.2 copy-start.12
  207.4 8.6 %copy-start.9 = (bf16[16,2,128,4,128]{2,4,3,1,0:T(8,128)(2,1)}, bf16[16,2,128,4,128]{2,4,3,1,0:T(8,128)(2,1)S(1)}, u32[]{:S(2)}) copy-start(bf16[16,2,128,4,128]{2,4,3,1,0:T(8,128)(2,1)S(1)} %copy.72) | copy-start | bytes 12582916
  208.0 8.0 %copy-start.13 = (bf16[896,512]{1,0:T(8,128)(2,1)S(1)}, bf16[896,512]{1,0:T(8,128)(2,1)}, u32[]{:S(2)}) copy-start(bf16[896,512]{1,0:T(8,128)(2,1)} %param.11) | copy-start | bytes 2752516
  298.0 125.1 %all-to-all-start.1 = ((bf16[32,64,896]{2,0,1:T(8,128)(2,1)}), bf16[32,64,896]{2,0,1:T(8,128)(2,1)}, u32[]{:S(2)}, u32[]{:S(2)}) async-start(bf16[32,64,896]{2,0,1:T(8,128)(2,1)} %copy.78), calls=%async_computation.2 | async-start | bytes 7340032 | tf_op jit(solution)/shard_map/all_to_all | solution.py:99
  304.1 206.7 %all-reduce.3.cloned.1.call-start = ((), (), s32[]{:S(2)}) async-start(), calls=%async_computation.5 | async-start | bytes 7340032 | tf_op jit(solution)/shard_map/psum | solution.py:107
  304.1 9.7 %copy-start.8 = (bf16[16,2,128,4,128]{2,4,3,1,0:T(8,128)(2,1)S(1)}, bf16[16,2,128,4,128]{2,4,3,1,0:T(8,128)(2,1)}, u32[]{:S(2)}) copy-start(bf16[16,2,128,4,128]{2,4,3,1,0:T(8,128)(2,1)} %copy-done.7) | copy-start | bytes 12582916
  321.5 6.4 %copy-start.4 = (bf16[16,4,64,2,128]{4,2,3,1,0:T(8,128)(2,1)S(1)}, bf16[16,4,64,2,128]{4,2,3,1,0:T(8,128)(2,1)}, u32[]{:S(2)}) copy-start(bf16[16,4,64,2,128]{4,2,3,1,0:T(8,128)(2,1)} %copy-done.3) | copy-start | bytes 6291460
  321.5 6.4 %copy-start.5 = (bf16[16,2,128,4,128]{4,3,2,1,0:T(4,128)(2,1)S(1)}, bf16[16,2,128,4,128]{4,3,2,1,0:T(4,128)(2,1)}, u32[]{:S(2)}) copy-start(bf16[16,2,128,4,128]{4,3,2,1,0:T(4,128)(2,1)} %reshape.170) | copy-start | bytes 12582916
  427.4 87.6 %copy-start.1 = (bf16[32,32,896]{2,1,0:T(8,128)(2,1)S(1)}, bf16[32,32,896]{2,1,0:T(8,128)(2,1)}, u32[]{:S(2)}) copy-start(bf16[32,32,896]{2,1,0:T(8,128)(2,1)} %param.9) | copy-start | bytes 5505028
  510.8 3.0 copy-start.10
Sparse Core Ops, SparseCore 0:
  107.7 53.4 all-gather.1
  225.9 65.3 reduce-scatter.1
  321.7 189.1 all-reduce.2
where the time goes:
time: 528 us; the launch traced here: 522 us
  waiting for transfers between devices  368 us (70%)
  matrix products  72.2 us (14%)
  local copies, waits for them, and re-layouts  44.4 us (8%)
  between operations  14.5 us (3%)
  starting transfers between devices  12.5 us (2%)
  other arithmetic  10.7 us (2%)
    all_to_all x1, waiting for transfers between devices, local(): lax.all_to_all(returning, 'seq', split_axis=1, concat_axis=1, tiled=True)  91.7 us
    all_to_all x1, waiting for transfers between devices, local(): lax.all_to_all(outgoing, 'seq', split_axis=0, concat_axis=0, tiled=True)  79.4 us
    psum x1, waiting for transfers between devices, local(): grad_w_key, grad_w_value = lax.psum((key_partial, value_partial), 'seq')  79.4 us
    reduce_scatter x1, waiting for transfers between devices, local(): lax.psum_scatter((jnp.einsum('jrc,ec->rje', grad_keys, w_key, preferred_e...  65.5 us
    all_gather x1, waiting for transfers between devices, local(): panel_piece = lax.all_gather(wanted, 'head', axis=1, tiled=True)  51.6 us
    dot_general x1, matrix products, local(): jnp.einsum('jre,ec->jrc', panel_piece, both_weights, preferred_element_ty...  11.7 us
  transfers between devices with their start and end apart: 5, of which 5 were waited for; matrix products, arithmetic and copies ran while one was open for 7% of the time, Pallas kernels for 0%

commit v1 on v0

v1 whole, which is shorter than its diff:
```python
import functools
import math

import jax
import jax.numpy as jnp
from jax import lax
from jax.experimental import pallas as pl
from jax.experimental.pallas import tpu as pltpu
from jax.sharding import PartitionSpec as P

DH = 128
STRETCH = 64
KNB = 2
CH_DEV = 16
ROW_CUTS = 2
COL_CUTS = (512, 384)


def chunk_list(rows, width):
    step = rows // ROW_CUTS
    pieces = []
    for cut in range(ROW_CUTS):
        start = 0
        for cols in COL_CUTS:
            pieces.append((cut * step, step, start, cols))
            start += cols
    assert start == width
    return pieces


def attention_kernel(pieces, shards, counts, *refs):
    n = len(pieces)
    q_ref, g_ref, wk_ref, wv_ref = refs[:4]
    panels = refs[4 : 4 + n]
    att_ref, gq_ref = refs[4 + n : 6 + n]
    shares = refs[6 + n : 6 + 2 * n]
    gk_ref, gv_ref, x_ref, dk_ref, dv_ref = refs[6 + 2 * n :]
    step = pl.program_id(0)
    f32, bf16 = jnp.float32, jnp.bfloat16
    rows_full = x_ref.shape[0] // KNB

    def places(k, first, count):
        begin = k * rows_full + first * shards
        return slice(begin, begin + count * shards)

    for (first, count, start, cols), ref in zip(pieces, panels):
        block = ref[...]
        for k in range(KNB):
            x_ref[places(k, first, count), start : start + cols] = block[:, k].reshape(
                shards * count, cols
            )
    x = x_ref[...]
    keys = jnp.dot(x, wk_ref[...], preferred_element_type=f32).astype(bf16)
    values = jnp.dot(x, wv_ref[...], preferred_element_type=f32).astype(bf16)
    factor = 1.0 / math.sqrt(DH)
    used = lax.broadcasted_iota(jnp.int32, (STRETCH, KNB * rows_full), 1) < (
        counts[step] * rows_full
    )
    across = (((1,), (1,)), ((), ()))
    down = (((0,), (0,)), ((), ()))
    for h in range(q_ref.shape[1] // DH):
        cols = slice(h * DH, (h + 1) * DH)
        q, g, key, value = q_ref[:, cols], g_ref[:, cols], keys[:, cols], values[:, cols]
        scores = lax.dot_general(q, key, across, preferred_element_type=f32) * factor
        scores = jnp.where(used, scores, -jnp.inf)
        exps = jnp.exp(scores - jnp.max(scores, axis=1, keepdims=True))
        probs = exps / jnp.sum(exps, axis=1, keepdims=True)
        weights = probs.astype(bf16)
        att_ref[:, cols] = jnp.dot(weights, value, preferred_element_type=f32).astype(bf16)
        dprobs = lax.dot_general(g, value, across, preferred_element_type=f32)
        row_dot = jnp.sum(probs * dprobs, axis=1, keepdims=True)
        dscores = (probs * (dprobs - row_dot)).astype(bf16)
        gq_ref[:, cols] = (jnp.dot(dscores, key, preferred_element_type=f32) * factor).astype(bf16)
        dk_ref[:, cols] = (
            lax.dot_general(dscores, q, down, preferred_element_type=f32) * factor
        ).astype(bf16)
        dv_ref[:, cols] = lax.dot_general(weights, g, down, preferred_element_type=f32).astype(bf16)
    dk, dv = dk_ref[...], dv_ref[...]
    share = (
        lax.dot_general(dk, wk_ref[...], across, preferred_element_type=f32)
        + lax.dot_general(dv, wv_ref[...], across, preferred_element_type=f32)
    ).astype(bf16)
    for (first, count, start, cols), ref in zip(pieces, shares):
        for k in range(KNB):
            ref[:, k] = share[places(k, first, count), start : start + cols].reshape(
                shards, count, cols
            )

    @pl.when(step == 0)
    def _():
        gk_ref[...] = jnp.zeros_like(gk_ref)
        gv_ref[...] = jnp.zeros_like(gv_ref)

    gk_ref[...] += lax.dot_general(x, dk, down, preferred_element_type=f32)
    gv_ref[...] += lax.dot_general(x, dv, down, preferred_element_type=f32)


def attention(pieces, shards, counts, queries, out_grad, w_key, w_value, panels):
    tokens, width = queries.shape
    enc_width = w_key.shape[0]
    requests = CH_DEV * KNB
    rows_full = shards * sum(p[1] for p in pieces if p[2] == 0)
    token_spec = pl.BlockSpec((STRETCH, width), lambda i, c: (i, 0))
    weight_spec = pl.BlockSpec((enc_width, width), lambda i, c: (0, 0))
    piece_specs = [
        pl.BlockSpec((shards, KNB, p[1], p[3]), lambda i, c: (0, i, 0, 0)) for p in pieces
    ]
    bf16 = jnp.bfloat16
    outs = (
        [jax.ShapeDtypeStruct((tokens, width), bf16)] * 2
        + [jax.ShapeDtypeStruct((shards, requests, p[1], p[3]), bf16) for p in pieces]
        + [jax.ShapeDtypeStruct((enc_width, width), jnp.float32)] * 2
    )
    all_rows = KNB * rows_full
    flops = CH_DEV * 2 * all_rows * width * (6 * enc_width + 6 * STRETCH)
    return pl.pallas_call(
        functools.partial(attention_kernel, pieces, shards),
        grid_spec=pltpu.PrefetchScalarGridSpec(
            num_scalar_prefetch=1,
            grid=(CH_DEV,),
            in_specs=[token_spec] * 2 + [weight_spec] * 2 + piece_specs,
            out_specs=[token_spec] * 2 + piece_specs + [weight_spec] * 2,
            scratch_shapes=[
                pltpu.VMEM((all_rows, enc_width), bf16),
                pltpu.VMEM((all_rows, width), bf16),
                pltpu.VMEM((all_rows, width), bf16),
            ],
        ),
        out_shape=outs,
        compiler_params=pltpu.CompilerParams(
            dimension_semantics=("arbitrary",), vmem_limit_bytes=48 * 1024 * 1024
        ),
        cost_estimate=pl.CostEstimate(
            flops=flops, bytes_accessed=32 * 1024 * 1024, transcendentals=0
        ),
    )(counts, queries, out_grad, w_key, w_value, *panels)


def local(queries, pool, w_key, w_value, out_grad, nb_source, nb_slot, nb_count):
    f32 = jnp.float32
    bf16 = jnp.bfloat16
    seq_count = lax.axis_size("seq")
    seq_index = lax.axis_index("seq")
    shards = lax.axis_size("head")
    requests = CH_DEV * KNB
    capacity = max(2, 2 * requests // seq_count)
    slot_span = seq_count * capacity
    source_table = nb_source.reshape(seq_count, requests)
    slot_table = nb_slot.reshape(seq_count, requests)
    order_ids = jnp.arange(requests)
    matches = source_table[:, :, None] == source_table[:, None, :]
    before = order_ids[None, :] < order_ids[:, None]
    ranks = jnp.sum(jnp.logical_and(matches, before[None, :, :]), axis=2)
    places = jnp.arange(capacity)
    chosen = jnp.logical_and(
        (source_table == seq_index)[:, :, None], ranks[:, :, None] == places[None, None, :]
    )
    picked_slot = jnp.sum(jnp.where(chosen, slot_table[:, :, None], 0), axis=1).reshape(slot_span)
    filled = jnp.any(chosen, axis=1).reshape(slot_span)
    own_sources = lax.dynamic_index_in_dim(source_table, seq_index, 0, keepdims=False)
    own_ranks = lax.dynamic_index_in_dim(ranks, seq_index, 0, keepdims=False)
    positions = own_sources * capacity + own_ranks
    pool_count, rows, enc_width = pool.shape
    pieces = chunk_list(rows, enc_width)
    used_counts = lax.dynamic_slice_in_dim(nb_count, seq_index * CH_DEV, CH_DEV)

    panels = []
    for first, count, start, cols in pieces:
        part = pool[:, first : first + count, start : start + cols]
        outgoing = jnp.take(part, picked_slot, axis=0, mode="clip")
        incoming = lax.all_to_all(outgoing, "seq", split_axis=0, concat_axis=0, tiled=True)
        wanted = jnp.take(incoming, positions, axis=0, mode="clip")
        panels.append(lax.all_gather(wanted, "head", axis=0, tiled=False))

    results = attention(
        pieces, shards, used_counts, queries, out_grad, w_key, w_value, panels
    )
    attended, grad_queries = results[:2]
    shares = results[2 : 2 + len(pieces)]
    key_partial, value_partial = results[2 + len(pieces) :]

    back = positions[None, :] == jnp.arange(slot_span)[:, None]
    back_index = jnp.sum(jnp.where(back, order_ids[None, :], 0), axis=1)
    collect = jnp.logical_and(
        picked_slot[None, :] == jnp.arange(pool_count)[:, None], filled[None, :]
    ).astype(bf16)
    grads = []
    for share in shares:
        summed = lax.psum_scatter(share, "head", scatter_dimension=0, tiled=False)
        returning = jnp.take(summed, back_index, axis=0, mode="clip")
        arrived = lax.all_to_all(returning, "seq", split_axis=0, concat_axis=0, tiled=True)
        grads.append(jnp.einsum("pq,qre->pre", collect, arrived, preferred_element_type=f32))
    columns = len(COL_CUTS)
    grad_pool = jnp.concatenate(
        [
            jnp.concatenate(grads[cut * columns : (cut + 1) * columns], axis=2)
            for cut in range(ROW_CUTS)
        ],
        axis=1,
    )
    grad_w_key, grad_w_value = lax.psum((key_partial, value_partial), "seq")
    return attended, grad_queries, grad_pool, grad_w_key, grad_w_value


def solution(mesh):
    return jax.shard_map(
        local,
        mesh=mesh,
        in_specs=(
            P("seq", "head"),
            P("seq", "head", None),
            P(None, "head"),
            P(None, "head"),
            P("seq", "head"),
            P(),
            P(),
            P(),
        ),
        out_specs=(
            P("seq", "head"),
            P("seq", "head"),
            P("seq", "head", None),
            P(None, "head"),
            P(None, "head"),
        ),
        check_vma=False,
    )
```

time: 528 us -> 529 us (level)
  blocking collectives: 0 us -> 82.8 us
  waiting for transfers between devices: 368 us -> 289 us
  matrix products: 72.2 us -> 4.93 us
  Pallas kernels: 0 us -> 66.2 us
  starting transfers between devices: 12.5 us -> 30.7 us
  other arithmetic: 10.7 us -> 1.15 us
  local copies, waits for them, and re-layouts: 44.4 us -> 36.3 us
    all_to_all x0 -> x3, blocking collectives: none -> 82.8 us  [local(): lax.all_to_all(outgoing, 'seq', split_axis=0, concat_axis=0, tiled=True)]
    dot_general x13 -> x4, matrix products: 72.2 us -> 4.93 us  [local(): jnp.einsum('pq,qre->pre', collect, arrived, preferred_element_type=f32)]
    pallas_call x0 -> x1, Pallas kernels: none -> 66.2 us  [attention(): pl.pallas_call(functools.partial(attention_kernel, pieces, shards), grid_...]
    all_to_all x1, waiting for transfers between devices: 79.4 us -> 18.5 us  [local(): lax.all_to_all(outgoing, 'seq', split_axis=0, concat_axis=0, tiled=True)]
    all_to_all x1 -> x4, waiting for transfers between devices: 91.7 us -> 44.2 us  [local(): lax.all_to_all(returning, 'seq', split_axis=0, concat_axis=0, tiled=True)]
    reduce_scatter x1 -> x4, waiting for transfers between devices: 65.5 us -> 98.1 us  [local(): summed = lax.psum_scatter(share, 'head', scatter_dimension=0, tiled=False)]
    all_gather x1 -> x4, waiting for transfers between devices: 51.6 us -> 22 us  [local(): panels.append(lax.all_gather(wanted, 'head', axis=0, tiled=False))]
    psum x1, waiting for transfers between devices: 79.4 us -> 104 us  [local(): grad_w_key, grad_w_value = lax.psum((key_partial, value_partial), 'seq')]
  transfers between devices with their start and end apart: 5 -> 14, of which waited for: 5 -> 8; matrix products, arithmetic and copies ran while one was open for 7% -> 6% of each run, Pallas kernels for 0% -> 0%
where the time goes in v1:
time: 529 us; the launch traced here: 525 us
  waiting for transfers between devices  289 us (55%)
  blocking collectives  82.8 us (16%)
  Pallas kernels  66.2 us (13%)
  local copies, waits for them, and re-layouts  36.3 us (7%)
  starting transfers between devices  30.7 us (6%)
  between operations  14 us (3%)
    psum x1, waiting for transfers between devices, local(): grad_w_key, grad_w_value = lax.psum((key_partial, value_partial), 'seq')  104 us
    reduce_scatter x4, waiting for transfers between devices, local(): summed = lax.psum_scatter(share, 'head', scatter_dimension=0, tiled=False)  98.1 us
    all_to_all x3, blocking collectives, local(): lax.all_to_all(outgoing, 'seq', split_axis=0, concat_axis=0, tiled=True)  82.8 us
    pallas_call x1, Pallas kernels, attention(): pl.pallas_call(functools.partial(attention_kernel, pieces, shards), grid_...  66.2 us
    all_to_all x4, waiting for transfers between devices, local(): lax.all_to_all(returning, 'seq', split_axis=0, concat_axis=0, tiled=True)  44.2 us
    all_to_all x4, starting transfers between devices, local(): lax.all_to_all(returning, 'seq', split_axis=0, concat_axis=0, tiled=True)  24.2 us
    all_gather x4, waiting for transfers between devices, local(): panels.append(lax.all_gather(wanted, 'head', axis=0, tiled=False))  22 us
    all_to_all x1, waiting for transfers between devices, local(): lax.all_to_all(outgoing, 'seq', split_axis=0, concat_axis=0, tiled=True)  18.5 us
  transfers between devices with their start and end apart: 14, of which 8 were waited for; matrix products, arithmetic and copies ran while one was open for 6% of the time, Pallas kernels for 0%

profile of v1, /device:TPU:8, one launch (start us, length us, event | category | flops | bytes accessed | tf_op | source)
XLA Modules:
  0.0 525.4 jit_solution(3099070397438501437)
XLA Ops:
  10.8 1.5 gather_fusion.6
  12.3 6.3 %all-to-all-start.3 = ((bf16[64,16,384]{2,1,0:T(8,128)(2,1)}), bf16[64,16,384]{2,1,0:T(8,128)(2,1)S(1)}, u32[]{:S(2)}, u32[]{:S(2)}) async-start(bf16[64,16,384]{2,1,0:T(8,128)(2,1)} %gather_fusion.6), calls=%async_computation.3 | async-start | bytes 1572864 | tf_op jit(solution)/shard_map/all_to_all | solution.py:171
  18.6 18.5 %all-to-all-done.3 = bf16[64,16,384]{2,1,0:T(8,128)(2,1)S(1)} async-done(((bf16[64,16,384]{2,1,0:T(8,128)(2,1)}), bf16[64,16,384]{2,1,0:T(8,128)(2,1)S(1)}, u32[]{:S(2)}, u32[]{:S(2)}) %all-to-all-start.3) | async-done | bytes 786464 | tf_op jit(solution)/shard_map/all_to_all | solution.py:171
  37.1 1.4 gather_fusion.7
  39.2 24.5 %all_to_all.40 = bf16[64,16,384]{2,1,0:T(8,128)(2,1)} all-to-all(bf16[64,16,384]{2,1,0:T(8,128)(2,1)S(1)} %gather_fusion.2), channel_id=1, replica_groups=mesh['seq'=8,'head'=4] {'seq'}, dimensions={0} | all-to-all | bytes 1572864 | tf_op jit(solution)/shard_map/all_to_all | solution.py:171
  63.8 2.5 gather_fusion.3
  67.1 28.8 %all_to_all.41 = bf16[64,16,512]{2,1,0:T(8,128)(2,1)S(1)} all-to-all(bf16[64,16,512]{2,1,0:T(8,128)(2,1)S(1)} %gather_fusion.4), channel_id=1, replica_groups=mesh['seq'=8,'head'=4] {'seq'}, dimensions={0} | all-to-all | bytes 2097152 | tf_op jit(solution)/shard_map/all_to_all | solution.py:171
  95.9 1.4 gather_fusion.5
  97.4 1.6 gather_fusion
  99.0 29.4 %all_to_all.42 = bf16[64,16,512]{2,1,0:T(8,128)(2,1)} all-to-all(bf16[64,16,512]{2,1,0:T(8,128)(2,1)} %gather_fusion), channel_id=1, replica_groups=mesh['seq'=8,'head'=4] {'seq'}, dimensions={0} | all-to-all | bytes 2097152 | tf_op jit(solution)/shard_map/all_to_all | solution.py:171
  128.4 2.6 gather_fusion.1
  131.2 22.0 %all-gather.9.cloned.1.call-done = bf16[128,16,512]{2,1,0:T(8,128)(2,1)} async-done(((bf16[32,16,512]{2,1,0:T(8,128)(2,1)}), bf16[128,16,512]{2,1,0:T(8,128)(2,1)}) %all-gather.9.cloned.1.call-update) | async-done | bytes 2097168 | tf_op jit(solution)/shard_map/all_gather | solution.py:173
  154.4 66.2 %shard_map.119 = (bf16[1024,512]{1,0:T(8,128)(2,1)}, bf16[1024,512]{1,0:T(8,128)(2,1)}, bf16[4,32,16,512]{3,2,1,0:T(8,128)(2,1)}, bf16[4,32,16,384]{3,2,1,0:T(8,...) custom-call(s32[16]{0:T(128)S(1)} %dynamic_slice.10.counts, ...), custom_call_target="tpu_custom_call" | custom-call | flops 24159191040 | bytes 33554432 | tf_op jit(solution)/shard_map/pallas_call | solution.py:116
  222.8 26.2 %reduce-scatter.11.cloned.1.call-done = bf16[1,32,16,384]{3,2,1,0:T(8,128)(2,1)} async-done(((bf16[4,32,16,384]{3,2,1,0:T(8,128)(2,1)}), bf16[1,32,16,384]{3,2,1,0:T(8,128)(2,1)}) %reduce-scatter.11.cloned.1.call-update) | async-done | bytes 393232 | tf_op jit(solution)/shard_map/reduce_scatter | solution.py:189
  248.9 2.5 gather_fusion.11
  251.5 6.0 %all-to-all-start.7 = ((bf16[64,16,384]{2,1,0:T(8,128)(2,1)}), bf16[64,16,384]{2,1,0:T(8,128)(2,1)S(1)}, u32[]{:S(2)}, u32[]{:S(2)}) async-start(bf16[64,16,384]{2,1,0:T(8,128)(2,1)} %gather_fusion.11), calls=%async_computation.11 | async-start | bytes 1572864 | tf_op jit(solution)/shard_map/all_to_all | solution.py:191
  257.5 22.2 %reduce-scatter.7.cloned.1.call-done = bf16[1,32,16,384]{3,2,1,0:T(8,128)(2,1)} async-done(((bf16[4,32,16,384]{3,2,1,0:T(8,128)(2,1)}), bf16[1,32,16,384]{3,2,1,0:T(8,128)(2,1)}) %reduce-scatter.7.cloned.1.call-update) | async-done | bytes 393232 | tf_op jit(solution)/shard_map/reduce_scatter | solution.py:189
  279.7 2.5 gather_fusion.9
  282.3 6.0 %all-to-all-start.5 = ((bf16[64,16,384]{2,1,0:T(8,128)(2,1)}), bf16[64,16,384]{2,1,0:T(8,128)(2,1)S(1)}, u32[]{:S(2)}, u32[]{:S(2)}) async-start(bf16[64,16,384]{2,1,0:T(8,128)(2,1)} %gather_fusion.9), calls=%async_computation.7 | async-start | bytes 1572864 | tf_op jit(solution)/shard_map/all_to_all | solution.py:191
  288.3 25.4 %reduce-scatter.9.cloned.1.call-done = bf16[1,32,16,512]{3,2,1,0:T(8,128)(2,1)} async-done(((bf16[4,32,16,512]{3,2,1,0:T(8,128)(2,1)}), bf16[1,32,16,512]{3,2,1,0:T(8,128)(2,1)}) %reduce-scatter.9.cloned.1.call-update) | async-done | bytes 524304 | tf_op jit(solution)/shard_map/reduce_scatter | solution.py:189
  313.7 2.6 gather_fusion.10
  317.3 6.0 %all-to-all-start.6 = ((bf16[64,16,512]{2,1,0:T(8,128)(2,1)}), bf16[64,16,512]{2,1,0:T(8,128)(2,1)S(1)}, u32[]{:S(2)}, u32[]{:S(2)}) async-start(bf16[64,16,512]{2,1,0:T(8,128)(2,1)} %gather_fusion.10), calls=%async_computation.9 | async-start | bytes 2097152 | tf_op jit(solution)/shard_map/all_to_all | solution.py:191
  324.0 24.4 %reduce-scatter.5.cloned.1.call-done = bf16[1,32,16,512]{3,2,1,0:T(8,128)(2,1)} async-done(((bf16[4,32,16,512]{3,2,1,0:T(8,128)(2,1)}), bf16[1,32,16,512]{3,2,1,0:T(8,128)(2,1)}) %reduce-scatter.5.cloned.1.call-update) | async-done | bytes 524304 | tf_op jit(solution)/shard_map/reduce_scatter | solution.py:189
  348.4 2.6 gather_fusion.8
  351.0 6.0 %all-to-all-start.4 = ((bf16[64,16,512]{2,1,0:T(8,128)(2,1)}), bf16[64,16,512]{2,1,0:T(8,128)(2,1)S(1)}, u32[]{:S(2)}, u32[]{:S(2)}) async-start(bf16[64,16,512]{2,1,0:T(8,128)(2,1)} %gather_fusion.8), calls=%async_computation.5 | async-start | bytes 2097152 | tf_op jit(solution)/shard_map/all_to_all | solution.py:191
  359.7 1.3 fusion
  361.1 44.2 %all-to-all-done.4 = bf16[64,16,512]{2,1,0:T(8,128)(2,1)S(1)} async-done(((bf16[64,16,512]{2,1,0:T(8,128)(2,1)}), bf16[64,16,512]{2,1,0:T(8,128)(2,1)S(1)}, u32[]{:S(2)}, u32[]{:S(2)}) %all-to-all-start.4) | async-done | bytes 1048608 | tf_op jit(solution)/shard_map/all_to_all | solution.py:191
  405.3 1.3 fusion.2
  406.9 4.0 copy.38
  410.9 103.7 %all-reduce.3.cloned.1.call-done = (f32[896,512]{1,0:T(8,128)}, f32[896,512]{1,0:T(8,128)}) async-done(((f32[896,512]{1,0:T(8,128)}, f32[896,512]{1,0:T(8,128)}), (f32[896,512]{1,0:T(8,128)}, f32[896,512]{1,0:T(8,128)})) %all-reduce.3.cloned.1.call-update) | async-done | bytes 3670032 | tf_op jit(solution)/shard_map/psum | solution.py:201
  514.6 3.0 copy.49
  517.6 1.2 copy.50
  (70 shorter events, 13.3 us)
Async XLA Ops:
  12.3 24.7 %all-to-all-start.3 = ((bf16[64,16,384]{2,1,0:T(8,128)(2,1)}), bf16[64,16,384]{2,1,0:T(8,128)(2,1)S(1)}, u32[]{:S(2)}, u32[]{:S(2)}) async-start(bf16[64,16,384]{2,1,0:T(8,128)(2,1)} %gather_fusion.6), calls=%async_computation.3 | async-start | bytes 1572864 | tf_op jit(solution)/shard_map/all_to_all | solution.py:171
  18.6 112.6 %all-gather.15.cloned.1.call-start = ((), (), s32[]{:S(2)}) async-start(), calls=%async_computation.19 | async-start | bytes 1966080 | tf_op jit(solution)/shard_map/all_gather | solution.py:173
  38.4 92.7 %all-gather.11.cloned.1.call-start = ((), (), s32[]{:S(2)}) async-start(), calls=%async_computation.17 | async-start | bytes 1966080 | tf_op jit(solution)/shard_map/all_gather | solution.py:173
  38.5 27.8 %copy-start.9 = (bf16[32,32,896]{2,1,0:T(8,128)(2,1)S(1)}, bf16[32,32,896]{2,1,0:T(8,128)(2,1)}, u32[]{:S(2)}) copy-start(bf16[32,32,896]{2,1,0:T(8,128)(2,1)} %param.9) | copy-start | bytes 5505028
  66.3 64.9 %all-gather.13.cloned.1.call-start = ((), (), s32[]{:S(2)}) async-start(), calls=%async_computation.18 | async-start | bytes 2621440 | tf_op jit(solution)/shard_map/all_gather | solution.py:173
  97.3 55.8 %all-gather.9.cloned.1.call-start = ((), (), s32[]{:S(2)}) async-start(), calls=%async_computation.16 | async-start | bytes 2621440 | tf_op jit(solution)/shard_map/all_gather | solution.py:173
  99.0 32.1 %copy-start.10 = (s32[128]{0:T(128)S(1)}, s32[128]{0:T(128)}, u32[]{:S(2)}) copy-start(s32[128]{0:T(128)} %param.15) | copy-start | bytes 1540
  99.0 54.2 %copy-start = (bf16[1024,512]{1,0:T(8,128)(2,1)S(1)}, bf16[1024,512]{1,0:T(8,128)(2,1)}, u32[]{:S(2)}) copy-start(bf16[1024,512]{1,0:T(8,128)(2,1)} %refs_0_.1) | copy-start | bytes 3145732
  99.0 54.2 %copy-start.1 = (bf16[1024,512]{1,0:T(8,128)(2,1)S(1)}, bf16[1024,512]{1,0:T(8,128)(2,1)}, u32[]{:S(2)}) copy-start(bf16[1024,512]{1,0:T(8,128)(2,1)} %refs_1_.1) | copy-start | bytes 3145732
  99.0 54.2 %copy-start.2 = (bf16[896,512]{1,0:T(8,128)(2,1)S(1)}, bf16[896,512]{1,0:T(8,128)(2,1)}, u32[]{:S(2)}) copy-start(bf16[896,512]{1,0:T(8,128)(2,1)} %refs_2_.1) | copy-start | bytes 2752516
  131.0 117.9 %reduce-scatter.11.cloned.1.call-start = ((), (), s32[]{:S(2)}) async-start(), calls=%async_computation.15 | async-start | bytes 1966080 | tf_op jit(solution)/shard_map/reduce_scatter | solution.py:189
  153.2 1.2 copy-start.3
  220.6 59.1 %reduce-scatter.7.cloned.1.call-start = ((), (), s32[]{:S(2)}) async-start(), calls=%async_computation.13 | async-start | bytes 1966080 | tf_op jit(solution)/shard_map/reduce_scatter | solution.py:189
  221.2 92.5 %reduce-scatter.9.cloned.1.call-start = ((), (), s32[]{:S(2)}) async-start(), calls=%async_computation.14 | async-start | bytes 2621440 | tf_op jit(solution)/shard_map/reduce_scatter | solution.py:189
  221.9 126.5 %reduce-scatter.5.cloned.1.call-start = ((), (), s32[]{:S(2)}) async-start(), calls=%async_computation.12 | async-start | bytes 2621440 | tf_op jit(solution)/shard_map/reduce_scatter | solution.py:189
  251.5 30.8 %all-to-all-start.7 = ((bf16[64,16,384]{2,1,0:T(8,128)(2,1)}), bf16[64,16,384]{2,1,0:T(8,128)(2,1)S(1)}, u32[]{:S(2)}, u32[]{:S(2)}) async-start(bf16[64,16,384]{2,1,0:T(8,128)(2,1)} %gather_fusion.11), calls=%async_computation.11 | async-start | bytes 1572864 | tf_op jit(solution)/shard_map/all_to_all | solution.py:191
  282.3 34.1 %all-to-all-start.5 = ((bf16[64,16,384]{2,1,0:T(8,128)(2,1)}), bf16[64,16,384]{2,1,0:T(8,128)(2,1)S(1)}, u32[]{:S(2)}, u32[]{:S(2)}) async-start(bf16[64,16,384]{2,1,0:T(8,128)(2,1)} %gather_fusion.9), calls=%async_computation.7 | async-start | bytes 1572864 | tf_op jit(solution)/shard_map/all_to_all | solution.py:191
  316.3 0.9 copy-start.6
  317.3 33.8 %all-to-all-start.6 = ((bf16[64,16,512]{2,1,0:T(8,128)(2,1)}), bf16[64,16,512]{2,1,0:T(8,128)(2,1)S(1)}, u32[]{:S(2)}, u32[]{:S(2)}) async-start(bf16[64,16,512]{2,1,0:T(8,128)(2,1)} %gather_fusion.10), calls=%async_computation.9 | async-start | bytes 2097152 | tf_op jit(solution)/shard_map/all_to_all | solution.py:191
  323.3 191.3 %all-reduce.3.cloned.1.call-start = ((), (), s32[]{:S(2)}) async-start(), calls=%async_computation.20 | async-start | bytes 7340032 | tf_op jit(solution)/shard_map/psum | solution.py:201
  351.0 54.2 %all-to-all-start.4 = ((bf16[64,16,512]{2,1,0:T(8,128)(2,1)}), bf16[64,16,512]{2,1,0:T(8,128)(2,1)S(1)}, u32[]{:S(2)}, u32[]{:S(2)}) async-start(bf16[64,16,512]{2,1,0:T(8,128)(2,1)} %gather_fusion.8), calls=%async_computation.5 | async-start | bytes 2097152 | tf_op jit(solution)/shard_map/all_to_all | solution.py:191
  357.4 1.2 copy-start.7
  361.1 45.5 %copy-start.4 = (f32[32,16,384]{2,0,1:T(8,128)S(1)}, f32[32,16,384]{2,0,1:T(8,128)}, u32[]{:S(2)}) copy-start(f32[32,16,384]{2,0,1:T(8,128)} %fusion.4) | copy-start | bytes 2359300
  405.3 1.3 copy-start.5
  514.6 3.0 copy-start.8
Sparse Core Ops, SparseCore 0:
  38.6 19.8 all-gather.14
  66.4 19.1 all-gather.10
  97.5 21.9 all-gather.12
  131.2 21.9 all-gather.8
  220.7 28.1 reduce-scatter.10
  251.5 28.1 reduce-scatter.6
  282.3 31.4 reduce-scatter.8
  317.0 31.3 reduce-scatter.4
  352.7 161.8 all-reduce.2

commit v2 on v1

--- a/solution.py
+++ b/solution.py
@@ -12,14 +12,14 @@
 STRETCH = 64
 KNB = 2
 CH_DEV = 16
-ROW_CUTS = 2
+ROW_TILE = 16
 COL_CUTS = (512, 384)
 
 
 def chunk_list(rows, width):
-    step = rows // ROW_CUTS
+    step = min(rows, ROW_TILE)
     pieces = []
-    for cut in range(ROW_CUTS):
+    for cut in range(rows // step):
         start = 0
         for cols in COL_CUTS:
             pieces.append((cut * step, step, start, cols))
@@ -136,6 +136,236 @@
     )(counts, queries, out_grad, w_key, w_value, *panels)
 
 
+MESH = pl.DeviceIdType.MESH
+
+
+def ring(axis):
+    size, me = lax.axis_size(axis), lax.axis_index(axis)
+    after = [lax.rem(me + o, size) for o in range(size)]
+    before = [lax.rem(me + size - o, size) for o in range(size)]
+    return size, me, after, before
+
+
+def greet(axes):
+    barrier = pltpu.get_barrier_semaphore()
+    total = 0
+    for axis in axes:
+        size, _, after, _ = ring(axis)
+        for o in range(1, size):
+            pl.semaphore_signal(barrier, inc=1, device_id={axis: after[o]}, device_id_type=MESH)
+        total += size - 1
+    pl.semaphore_wait(barrier, total)
+
+
+class Exchange:
+    def __init__(self, axis, source, target, send, recv, own):
+        self.size, me, after, before = ring(axis)
+        self.own = pltpu.make_async_copy(source(me), target(me), own)
+        others = range(1, self.size)
+
+        def copy(o, place):
+            return pltpu.make_async_remote_copy(
+                src_ref=source(after[o]),
+                dst_ref=target(place),
+                send_sem=send.at[o],
+                recv_sem=recv.at[o],
+                device_id={axis: after[o]},
+                device_id_type=MESH,
+            )
+
+        self.outward = [copy(o, me) for o in others]
+        self.inward = [copy(o, before[o]) for o in others]
+
+    def start(self):
+        for copy in self.outward:
+            copy.start()
+        self.own.start()
+
+    def wait_recv(self):
+        for copy in self.inward:
+            copy.wait_recv()
+        self.own.wait()
+
+    def wait_send(self):
+        for copy in self.outward:
+            copy.wait_send()
+
+
+def fetch_kernel(pieces, capacity, picked, positions, pool, *refs):
+    n = len(pieces)
+    panels, outgoing, incoming, wanted = (refs[i * n : (i + 1) * n] for i in range(4))
+    seq_send, seq_recv, seq_own, head_send, head_recv, head_own = refs[4 * n :]
+    requests = wanted[0].shape[0]
+    slots = outgoing[0].shape[0]
+
+    def select(p):
+        first, count, start, cols = pieces[p]
+
+        def body(j, carry):
+            outgoing[p][j] = pool[picked[j], first : first + count, start : start + cols]
+            return carry
+
+        lax.fori_loop(0, slots, body, 0)
+
+    def crossing(p):
+        return Exchange(
+            "seq",
+            lambda d: outgoing[p].at[pl.ds(d * capacity, capacity)],
+            lambda d: incoming[p].at[pl.ds(d * capacity, capacity)],
+            seq_send.at[p],
+            seq_recv.at[p],
+            seq_own.at[p],
+        )
+
+    def spreading(p):
+        return Exchange(
+            "head",
+            lambda d: wanted[p],
+            lambda d: panels[p].at[d],
+            head_send.at[p],
+            head_recv.at[p],
+            head_own.at[p],
+        )
+
+    crossings = [crossing(p) for p in range(n)]
+    spreadings = [spreading(p) for p in range(n)]
+    select(0)
+    greet(("seq", "head"))
+    crossings[0].start()
+    for p in range(1, n):
+        select(p)
+        if p == 1:
+            crossings[p].start()
+    for p in range(n):
+        crossings[p].wait_recv()
+        crossings[p].wait_send()
+        if p + 2 < n:
+            crossings[p + 2].start()
+
+        def body(j, carry):
+            wanted[p][j] = incoming[p][positions[j]]
+            return carry
+
+        lax.fori_loop(0, requests, body, 0)
+        spreadings[p].start()
+    for p in range(n):
+        spreadings[p].wait_send()
+        spreadings[p].wait_recv()
+
+
+def return_kernel(pieces, capacity, back, *refs):
+    n = len(pieces)
+    shares, arrived, got, summed, returning = (refs[i * n : (i + 1) * n] for i in range(5))
+    seq_send, seq_recv, seq_own, head_send, head_recv, head_own = refs[5 * n :]
+    shards, requests = got[0].shape[:2]
+    slots = returning[0].shape[0]
+
+    def gathering(p):
+        return Exchange(
+            "head",
+            lambda d: shares[p].at[d],
+            lambda d: got[p].at[d],
+            head_send.at[p],
+            head_recv.at[p],
+            head_own.at[p],
+        )
+
+    def crossing(p):
+        return Exchange(
+            "seq",
+            lambda d: returning[p].at[pl.ds(d * capacity, capacity)],
+            lambda d: arrived[p].at[pl.ds(d * capacity, capacity)],
+            seq_send.at[p],
+            seq_recv.at[p],
+            seq_own.at[p],
+        )
+
+    gatherings = [gathering(p) for p in range(n)]
+    crossings = [crossing(p) for p in range(n)]
+    greet(("seq", "head"))
+    for p in range(min(2, n)):
+        gatherings[p].start()
+    for p in range(n):
+        gatherings[p].wait_recv()
+        gatherings[p].wait_send()
+        if p + 2 < n:
+            gatherings[p + 2].start()
+
+        def add(j, carry):
+            total = got[p][0, j].astype(jnp.float32)
+            for g in range(1, shards):
+                total += got[p][g, j].astype(jnp.float32)
+            summed[p][j] = total.astype(jnp.bfloat16)
+            return carry
+
+        def place(j, carry):
+            returning[p][j] = summed[p][back[j]]
+            return carry
+
+        lax.fori_loop(0, requests, add, 0)
+        lax.fori_loop(0, slots, place, 0)
+        crossings[p].start()
+    for p in range(n):
+        crossings[p].wait_send()
+        crossings[p].wait_recv()
+
+
+def semaphores(n, seq_count, shards):
+    dma = pltpu.SemaphoreType.DMA
+    return [
+        dma((n, seq_count)),
+        dma((n, seq_count)),
+        dma((n,)),
+        dma((n, shards)),
+        dma((n, shards)),
+        dma((n,)),
+    ]
+
+
+def fetch(pieces, capacity, seq_count, shards, picked, positions, pool):
+    bf16 = jnp.bfloat16
+    slots, requests = picked.shape[0], positions.shape[0]
+    smem = pl.BlockSpec(memory_space=pltpu.SMEM)
+    return pl.pallas_call(
+        functools.partial(fetch_kernel, pieces, capacity),
+        out_shape=[jax.ShapeDtypeStruct((shards, requests, p[1], p[3]), bf16) for p in pieces],
+        in_specs=[smem, smem, pl.BlockSpec(memory_space=pltpu.VMEM)],
+        out_specs=[pl.BlockSpec(memory_space=pl.ANY)] * len(pieces),
+        scratch_shapes=[pltpu.VMEM((slots, p[1], p[3]), bf16) for p in pieces]
+        + [pltpu.VMEM((slots, p[1], p[3]), bf16) for p in pieces]
+        + [pltpu.VMEM((requests, p[1], p[3]), bf16) for p in pieces]
+        + semaphores(len(pieces), seq_count, shards),
+        compiler_params=pltpu.CompilerParams(
+            collective_id=0, has_side_effects=True, vmem_limit_bytes=40 * 1024 * 1024
+        ),
+        cost_estimate=pl.CostEstimate(
+            flops=0, bytes_accessed=256 * 1024 * 1024, transcendentals=0
+        ),
+    )(picked, positions, pool)
+
+
+def give_back(pieces, capacity, seq_count, shards, back, shares):
+    bf16 = jnp.bfloat16
+    slots, requests = back.shape[0], shares[0].shape[1]
+    hbm = pl.BlockSpec(memory_space=pl.ANY)
+    return pl.pallas_call(
+        functools.partial(return_kernel, pieces, capacity),
+        out_shape=[jax.ShapeDtypeStruct((slots, p[1], p[3]), bf16) for p in pieces],
+        in_specs=[pl.BlockSpec(memory_space=pltpu.SMEM)] + [hbm] * len(pieces),
+        out_specs=[hbm] * len(pieces),
+        scratch_shapes=[pltpu.VMEM((shards, requests, p[1], p[3]), bf16) for p in pieces]
+        + [pltpu.VMEM((requests, p[1], p[3]), bf16) for p in pieces]
+        + [pltpu.VMEM((slots, p[1], p[3]), bf16) for p in pieces]
+        + semaphores(len(pieces), seq_count, shards),
+        compiler_params=pltpu.CompilerParams(
+            collective_id=1, has_side_effects=True, vmem_limit_bytes=40 * 1024 * 1024
+        ),
+        cost_estimate=pl.CostEstimate(
+            flops=0, bytes_accessed=256 * 1024 * 1024, transcendentals=0
+        ),
+    )(back, *shares)
+
+
 def local(queries, pool, w_key, w_value, out_grad, nb_source, nb_slot, nb_count):
     f32 = jnp.float32
     bf16 = jnp.bfloat16
@@ -164,14 +394,7 @@
     pieces = chunk_list(rows, enc_width)
     used_counts = lax.dynamic_slice_in_dim(nb_count, seq_index * CH_DEV, CH_DEV)
 
-    panels = []
-    for first, count, start, cols in pieces:
-        part = pool[:, first : first + count, start : start + cols]
-        outgoing = jnp.take(part, picked_slot, axis=0, mode="clip")
-        incoming = lax.all_to_all(outgoing, "seq", split_axis=0, concat_axis=0, tiled=True)
-        wanted = jnp.take(incoming, positions, axis=0, mode="clip")
-        panels.append(lax.all_gather(wanted, "head", axis=0, tiled=False))
-
+    panels = fetch(pieces, capacity, seq_count, shards, picked_slot, positions, pool)
     results = attention(
         pieces, shards, used_counts, queries, out_grad, w_key, w_value, panels
     )
@@ -184,17 +407,15 @@
     collect = jnp.logical_and(
         picked_slot[None, :] == jnp.arange(pool_count)[:, None], filled[None, :]
     ).astype(bf16)
-    grads = []
-    for share in shares:
-        summed = lax.psum_scatter(share, "head", scatter_dimension=0, tiled=False)
-        returning = jnp.take(summed, back_index, axis=0, mode="clip")
-        arrived = lax.all_to_all(returning, "seq", split_axis=0, concat_axis=0, tiled=True)
-        grads.append(jnp.einsum("pq,qre->pre", collect, arrived, preferred_element_type=f32))
+    arrived = give_back(pieces, capacity, seq_count, shards, back_index, shares)
+    grads = [
+        jnp.einsum("pq,qre->pre", collect, part, preferred_element_type=f32) for part in arrived
+    ]
     columns = len(COL_CUTS)
     grad_pool = jnp.concatenate(
         [
             jnp.concatenate(grads[cut * columns : (cut + 1) * columns], axis=2)
-            for cut in range(ROW_CUTS)
+            for cut in range(len(pieces) // columns)
         ],
         axis=1,
     )

time: 529 us -> 424 us (0.80)
  Pallas kernels: 66.2 us -> 333 us
  waiting for transfers between devices: 289 us -> 40 us
  blocking collectives: 82.8 us -> 0 us
  starting transfers between devices: 30.7 us -> 0.04 us
  local copies, waits for them, and re-layouts: 36.3 us -> 28.8 us
    pallas_call x0 -> x2, Pallas kernels: none -> 266 us  [the longest x1 151 us: give_back(): pl.pallas_call(functools.partial(return_kernel, pieces, capacity), out_sh...]
    reduce_scatter x4 -> x0, waiting for transfers between devices: 98.1 us -> none  [local(): summed = lax.psum_scatter(share, 'head', scatter_dimension=0, tiled=False)]
    all_to_all x3 -> x0, blocking collectives: 82.8 us -> none  [local(): lax.all_to_all(outgoing, 'seq', split_axis=0, concat_axis=0, tiled=True)]
    psum x1, waiting for transfers between devices: 104 us -> 40 us  [local(): grad_w_key, grad_w_value = lax.psum((key_partial, value_partial), 'seq')]
    all_to_all x5 -> x0, waiting for transfers between devices: 62.7 us -> none  [the longest x4 44.2 us: local(): lax.all_to_all(returning, 'seq', split_axis=0, concat_axis=0, tiled=True)]
    all_to_all x5 -> x0, starting transfers between devices: 30.4 us -> none  [the longest x4 24.2 us: local(): lax.all_to_all(returning, 'seq', split_axis=0, concat_axis=0, tiled=True)]
    gather x12 -> x0, local copies, waits for them, and re-layouts: 22.6 us -> none  [the longest x4 10.3 us: local(): returning = jnp.take(summed, back_index, axis=0, mode='clip')]
    all_gather x4 -> x0, waiting for transfers between devices: 22 us -> none  [local(): panels.append(lax.all_gather(wanted, 'head', axis=0, tiled=False))]
  transfers between devices with their start and end apart: 14 -> 1, of which waited for: 8 -> 1; matrix products, arithmetic and copies ran while one was open for 6% -> 2% of each run, Pallas kernels for 0% -> 36%
where the time goes in v2:
time: 424 us; the launch traced here: 420 us
  Pallas kernels  333 us (79%)
  waiting for transfers between devices  40 us (9%)
  local copies, waits for them, and re-layouts  28.8 us (7%)
  between operations  14.2 us (3%)
    pallas_call x1, Pallas kernels, give_back(): pl.pallas_call(functools.partial(return_kernel, pieces, capacity), out_sh...  151 us
    pallas_call x1, Pallas kernels, fetch(): pl.pallas_call(functools.partial(fetch_kernel, pieces, capacity), out_sha...  116 us
    pallas_call x1, Pallas kernels, attention(): pl.pallas_call(functools.partial(attention_kernel, pieces, shards), grid_...  66.6 us
    psum x1, waiting for transfers between devices, local(): grad_w_key, grad_w_value = lax.psum((key_partial, value_partial), 'seq')  40 us
    unnamed x35, local copies, waits for them, and re-layouts  27.7 us
  transfers between devices with their start and end apart: 1, of which 1 were waited for; matrix products, arithmetic and copies ran while one was open for 2% of the time, Pallas kernels for 36%

profile of v2, /device:TPU:8, one launch (start us, length us, event | category | flops | bytes accessed | tf_op | source)
XLA Modules:
  0.0 420.2 jit_solution(14461049034740540294)
XLA Ops:
  7.2 0.8 copy.25
  8.1 0.3 convert_reduce_fusion
  8.4 0.8 copy.26
  9.3 0.2 select_reduce_fusion
  9.6 0.7 dynamic_slice.10.counts
  10.4 1.5 copy-done.2
  11.9 115.5 %shard_map.119 = (bf16[4,32,16,512]{3,2,1,0:T(8,128)(2,1)S(1)}, bf16[4,32,16,384]{3,2,1,0:T(8,128)(2,1)S(1)}, bf16[4,32,16,512]{3,2,1,0:T(8,128)(2,1)S(1)}, bf16[4,32,16,384]{3,2,1,0:T(8,128)(2,1)S(1)}) custom-call(s32[64]{0:T(128)S(1)} %reshape.43.picked, s32[32]{0:T(128)S(1)} %add_bitcast_fusion.positions, bf16[32,32,896]{2,1,0:T(8,128)(2,1)S(1)} %copy-done.2), custom_call_target="tpu_custom_call" | custom-call | bytes 268435456 | tf_op jit(solution)/shard_map/pallas_call | solution.py:329
  127.4 1.3 copy-done.6
  128.7 1.3 copy-done.7
  130.0 1.1 copy-done.8
  131.2 1.2 copy-done.9
  132.3 1.2 copy-done.10
  133.6 1.2 copy-done.11
  134.8 1.2 copy-done.12
  136.0 1.2 copy-done.13
  137.2 66.6 %shard_map.120 = (bf16[1024,512]{1,0:T(8,128)(2,1)}, bf16[1024,512]{1,0:T(8,128)(2,1)}, bf16[4,32,16,512]{3,2,1,0:T(8,128)(2,1)}, bf16[4,32,16,384]{3,2,1,0:T(8,...) custom-call(s32[16]{0:T(128)S(1)} %dynamic_slice.10.counts, ...), custom_call_target="tpu_custom_call" | custom-call | flops 24159191040 | bytes 33554432 | tf_op jit(solution)/shard_map/pallas_call | solution.py:116
  203.7 1.1 copy-done.3
  204.9 0.2 fusion.9
  205.3 1.2 copy-done
  206.5 1.6 copy-done.1
  208.1 1.4 copy-done.4
  209.5 1.4 copy-done.5
  210.9 150.8 %shard_map.121 = (bf16[64,16,512]{2,1,0:T(8,128)(2,1)S(1)}, bf16[64,16,384]{2,1,0:T(8,128)(2,1)S(1)}, bf16[64,16,512]{2,1,0:T(8,128)(2,1)S(1)}, bf16[64,16,384]{2,1,0:T(8,128)(2,1)S(1)}) custom-call(s32[64]{0:T(128)S(1)} %select_reduce_fusion.1.back, bf16[4,32,16,512]{3,2,1,0:T(8,128)(2,1)S(1)} %copy-done, bf16[4,32,16,384]{3,2,1,0:T(8,128)(2,1)S(1)} %copy-done.4, ...), custom_call_target="tpu_custom_call" | custom-call | bytes 268435456 | tf_op jit(solution)/shard_map/pallas_call | solution.py:351
  361.7 0.3 fusion.6
  362.0 0.3 fusion.4
  362.2 1.3 fusion.2
  363.5 1.3 fusion
  364.9 0.3 maximum_maximum_fusion
  365.2 4.0 copy.31
  369.2 40.0 %all-reduce.3.cloned.1.call-done = (f32[896,512]{1,0:T(8,128)}, f32[896,512]{1,0:T(8,128)}) async-done(((f32[896,512]{1,0:T(8,128)}, f32[896,512]{1,0:T(8,128)}), (f32[896,512]{1,0:T(8,128)}, f32[896,512]{1,0:T(8,128)})) %all-reduce.3.cloned.1.call-update) | async-done | bytes 3670032 | tf_op jit(solution)/shard_map/psum | solution.py:422
  409.1 3.0 copy.42
  412.1 1.2 copy.43
  (26 shorter events, 0.6 us)
Async XLA Ops:
  7.2 402.0 %all-reduce.3.cloned.1.call-start = ((), (), s32[]{:S(2)}) async-start(), calls=%async_computation | async-start | bytes 7340032 | tf_op jit(solution)/shard_map/psum | solution.py:422
  10.4 1.5 copy-start.2
  127.4 1.3 copy-start.6
  128.7 1.3 copy-start.7
  130.0 1.1 copy-start.8
  131.2 1.2 copy-start.9
  132.3 1.2 copy-start.10
  133.6 1.2 copy-start.11
  134.8 1.2 copy-start.12
  136.0 1.2 copy-start.13
  203.7 1.1 copy-start.3
  204.9 1.6 copy-start
  206.5 1.6 copy-start.1
  208.1 1.4 copy-start.4
  209.5 1.4 copy-start.5
  409.1 3.0 copy-start.14
Sparse Core Ops, SparseCore 0:
  205.0 204.0 all-reduce.2

commit v3 on v2

--- a/solution.py
+++ b/solution.py
@@ -12,6 +12,8 @@
 STRETCH = 64
 KNB = 2
 CH_DEV = 16
+GROUP = 4
+VMEM_LIMIT = 60 * 1024 * 1024
 ROW_TILE = 16
 COL_CUTS = (512, 384)
 
@@ -34,10 +36,12 @@
     panels = refs[4 : 4 + n]
     att_ref, gq_ref = refs[4 + n : 6 + n]
     shares = refs[6 + n : 6 + 2 * n]
-    gk_ref, gv_ref, x_ref, dk_ref, dv_ref = refs[6 + 2 * n :]
+    gw_ref, x_ref, d_ref = refs[6 + 2 * n :]
     step = pl.program_id(0)
     f32, bf16 = jnp.float32, jnp.bfloat16
-    rows_full = x_ref.shape[0] // KNB
+    rows_full = x_ref.shape[0] // (GROUP * KNB)
+    width = q_ref.shape[1]
+    span = KNB * rows_full
 
     def places(k, first, count):
         begin = k * rows_full + first * shards
@@ -45,7 +49,7 @@
 
     for (first, count, start, cols), ref in zip(pieces, panels):
         block = ref[...]
-        for k in range(KNB):
+        for k in range(GROUP * KNB):
             x_ref[places(k, first, count), start : start + cols] = block[:, k].reshape(
                 shards * count, cols
             )
@@ -53,46 +57,52 @@
     keys = jnp.dot(x, wk_ref[...], preferred_element_type=f32).astype(bf16)
     values = jnp.dot(x, wv_ref[...], preferred_element_type=f32).astype(bf16)
     factor = 1.0 / math.sqrt(DH)
-    used = lax.broadcasted_iota(jnp.int32, (STRETCH, KNB * rows_full), 1) < (
-        counts[step] * rows_full
-    )
+    column = lax.broadcasted_iota(jnp.int32, (STRETCH, span), 1)
     across = (((1,), (1,)), ((), ()))
     down = (((0,), (0,)), ((), ()))
-    for h in range(q_ref.shape[1] // DH):
-        cols = slice(h * DH, (h + 1) * DH)
-        q, g, key, value = q_ref[:, cols], g_ref[:, cols], keys[:, cols], values[:, cols]
-        scores = lax.dot_general(q, key, across, preferred_element_type=f32) * factor
-        scores = jnp.where(used, scores, -jnp.inf)
-        exps = jnp.exp(scores - jnp.max(scores, axis=1, keepdims=True))
-        probs = exps / jnp.sum(exps, axis=1, keepdims=True)
-        weights = probs.astype(bf16)
-        att_ref[:, cols] = jnp.dot(weights, value, preferred_element_type=f32).astype(bf16)
-        dprobs = lax.dot_general(g, value, across, preferred_element_type=f32)
-        row_dot = jnp.sum(probs * dprobs, axis=1, keepdims=True)
-        dscores = (probs * (dprobs - row_dot)).astype(bf16)
-        gq_ref[:, cols] = (jnp.dot(dscores, key, preferred_element_type=f32) * factor).astype(bf16)
-        dk_ref[:, cols] = (
-            lax.dot_general(dscores, q, down, preferred_element_type=f32) * factor
-        ).astype(bf16)
-        dv_ref[:, cols] = lax.dot_general(weights, g, down, preferred_element_type=f32).astype(bf16)
-    dk, dv = dk_ref[...], dv_ref[...]
+    for c in range(GROUP):
+        used = column < counts[step * GROUP + c] * rows_full
+        tokens, rows = slice(c * STRETCH, (c + 1) * STRETCH), slice(c * span, (c + 1) * span)
+        for h in range(width // DH):
+            cols = slice(h * DH, (h + 1) * DH)
+            q, g = q_ref[tokens, cols], g_ref[tokens, cols]
+            key, value = keys[rows, cols], values[rows, cols]
+            scores = lax.dot_general(q, key, across, preferred_element_type=f32) * factor
+            scores = jnp.where(used, scores, -jnp.inf)
+            exps = jnp.exp(scores - jnp.max(scores, axis=1, keepdims=True))
+            probs = exps / jnp.sum(exps, axis=1, keepdims=True)
+            weights = probs.astype(bf16)
+            att_ref[tokens, cols] = jnp.dot(weights, value, preferred_element_type=f32).astype(bf16)
+            dprobs = lax.dot_general(g, value, across, preferred_element_type=f32)
+            row_dot = jnp.sum(probs * dprobs, axis=1, keepdims=True)
+            dscores = (probs * (dprobs - row_dot)).astype(bf16)
+            gq_ref[tokens, cols] = (
+                jnp.dot(dscores, key, preferred_element_type=f32) * factor
+            ).astype(bf16)
+            d_ref[rows, cols] = (
+                lax.dot_general(dscores, q, down, preferred_element_type=f32) * factor
+            ).astype(bf16)
+            d_ref[rows, width + h * DH : width + (h + 1) * DH] = lax.dot_general(
+                weights, g, down, preferred_element_type=f32
+            ).astype(bf16)
+    both = d_ref[...]
     share = (
-        lax.dot_general(dk, wk_ref[...], across, preferred_element_type=f32)
-        + lax.dot_general(dv, wv_ref[...], across, preferred_element_type=f32)
+        lax.dot_general(both[:, :width], wk_ref[...], across, preferred_element_type=f32)
+        + lax.dot_general(both[:, width:], wv_ref[...], across, preferred_element_type=f32)
     ).astype(bf16)
     for (first, count, start, cols), ref in zip(pieces, shares):
-        for k in range(KNB):
+        for k in range(GROUP * KNB):
             ref[:, k] = share[places(k, first, count), start : start + cols].reshape(
                 shards, count, cols
             )
 
     @pl.when(step == 0)
     def _():
-        gk_ref[...] = jnp.zeros_like(gk_ref)
-        gv_ref[...] = jnp.zeros_like(gv_ref)
-
-    gk_ref[...] += lax.dot_general(x, dk, down, preferred_element_type=f32)
-    gv_ref[...] += lax.dot_general(x, dv, down, preferred_element_type=f32)
+        gw_ref[...] = jnp.zeros_like(gw_ref)
+
+    partial = lax.dot_general(x, both, down, preferred_element_type=f32)
+    gw_ref[0] += partial[:, :width]
+    gw_ref[1] += partial[:, width:]
 
 
 def attention(pieces, shards, counts, queries, out_grad, w_key, w_value, panels):
@@ -100,35 +110,36 @@
     enc_width = w_key.shape[0]
     requests = CH_DEV * KNB
     rows_full = shards * sum(p[1] for p in pieces if p[2] == 0)
-    token_spec = pl.BlockSpec((STRETCH, width), lambda i, c: (i, 0))
+    token_spec = pl.BlockSpec((GROUP * STRETCH, width), lambda i, c: (i, 0))
     weight_spec = pl.BlockSpec((enc_width, width), lambda i, c: (0, 0))
     piece_specs = [
-        pl.BlockSpec((shards, KNB, p[1], p[3]), lambda i, c: (0, i, 0, 0)) for p in pieces
+        pl.BlockSpec((shards, GROUP * KNB, p[1], p[3]), lambda i, c: (0, i, 0, 0)) for p in pieces
     ]
     bf16 = jnp.bfloat16
     outs = (
         [jax.ShapeDtypeStruct((tokens, width), bf16)] * 2
         + [jax.ShapeDtypeStruct((shards, requests, p[1], p[3]), bf16) for p in pieces]
-        + [jax.ShapeDtypeStruct((enc_width, width), jnp.float32)] * 2
-    )
-    all_rows = KNB * rows_full
-    flops = CH_DEV * 2 * all_rows * width * (6 * enc_width + 6 * STRETCH)
+        + [jax.ShapeDtypeStruct((2, enc_width, width), jnp.float32)]
+    )
+    all_rows = GROUP * KNB * rows_full
+    flops = CH_DEV // GROUP * 2 * all_rows * width * (6 * enc_width + 6 * STRETCH)
     return pl.pallas_call(
         functools.partial(attention_kernel, pieces, shards),
         grid_spec=pltpu.PrefetchScalarGridSpec(
             num_scalar_prefetch=1,
-            grid=(CH_DEV,),
+            grid=(CH_DEV // GROUP,),
             in_specs=[token_spec] * 2 + [weight_spec] * 2 + piece_specs,
-            out_specs=[token_spec] * 2 + piece_specs + [weight_spec] * 2,
+            out_specs=[token_spec] * 2
+            + piece_specs
+            + [pl.BlockSpec((2, enc_width, width), lambda i, c: (0, 0, 0))],
             scratch_shapes=[
                 pltpu.VMEM((all_rows, enc_width), bf16),
-                pltpu.VMEM((all_rows, width), bf16),
-                pltpu.VMEM((all_rows, width), bf16),
+                pltpu.VMEM((all_rows, 2 * width), bf16),
             ],
         ),
         out_shape=outs,
         compiler_params=pltpu.CompilerParams(
-            dimension_semantics=("arbitrary",), vmem_limit_bytes=48 * 1024 * 1024
+            dimension_semantics=("arbitrary",), vmem_limit_bytes=VMEM_LIMIT
         ),
         cost_estimate=pl.CostEstimate(
             flops=flops, bytes_accessed=32 * 1024 * 1024, transcendentals=0
@@ -253,10 +264,16 @@
         spreadings[p].wait_recv()
 
 
-def return_kernel(pieces, capacity, back, *refs):
+def return_kernel(pieces, capacity, back, partial, *refs):
     n = len(pieces)
-    shares, arrived, got, summed, returning = (refs[i * n : (i + 1) * n] for i in range(5))
-    seq_send, seq_recv, seq_own, head_send, head_recv, head_own = refs[5 * n :]
+    shares, arrived = refs[:n], refs[n : 2 * n]
+    weights = refs[2 * n]
+    got, summed, returning = (refs[2 * n + 1 + i * n : 2 * n + 1 + (i + 1) * n] for i in range(3))
+    seq_send, seq_recv, seq_own, head_send, head_recv, head_own = refs[5 * n + 1 : 5 * n + 7]
+    half, half_in, mine, mine_in, pair_sem, sum_send, sum_recv, all_send, all_recv = refs[
+        5 * n + 7 :
+    ]
+    f32, bf16 = jnp.float32, jnp.bfloat16
     shards, requests = got[0].shape[:2]
     slots = returning[0].shape[0]
 
@@ -280,11 +297,87 @@
             seq_own.at[p],
         )
 
+    me, size = lax.axis_index("seq"), lax.axis_size("seq")
+    pairs = size // 2
+    side, rank = lax.rem(me, 2), lax.div(me, 2)
+
+    def to_seq(src, dst, send, recv, device):
+        return pltpu.make_async_remote_copy(
+            src_ref=src,
+            dst_ref=dst,
+            send_sem=send,
+            recv_sem=recv,
+            device_id={"seq": device},
+            device_id_type=MESH,
+        )
+
+    def at(o):
+        return lax.rem(rank + o, pairs)
+
+    others = range(1, pairs)
+    partner = 2 * rank + 1 - side
+    halving = to_seq(half, half_in, pair_sem.at[0], pair_sem.at[1], partner)
+    doubling = to_seq(weights.at[side], weights.at[side], pair_sem.at[2], pair_sem.at[3], partner)
+    doubled = to_seq(
+        weights.at[side], weights.at[1 - side], pair_sem.at[2], pair_sem.at[3], partner
+    )
+    sums = [
+        to_seq(mine.at[at(o)], mine_in.at[o], sum_send.at[o], sum_recv.at[o], 2 * at(o) + side)
+        for o in others
+    ]
+
+    def sharing(o, place):
+        return to_seq(
+            weights.at[side, rank],
+            weights.at[side, place],
+            all_send.at[o],
+            all_recv.at[o],
+            2 * at(o) + side,
+        )
+
+    shared_out = [sharing(o, rank) for o in others]
+    shared_in = [sharing(o, at(pairs - o)) for o in others]
+
+    def first_sum():
+        halving.wait_recv()
+
+        def body(j, carry):
+            mine[j] = (partial[side, j] + half_in[j].astype(f32)).astype(bf16)
+            return carry
+
+        lax.fori_loop(0, pairs, body, 0)
+        for copy in sums:
+            copy.start()
+
+    def second_sum():
+        total = partial[side, rank] + half_in[rank].astype(f32)
+        for o, copy in zip(others, sums):
+            copy.wait_recv()
+            total += mine_in[o].astype(f32)
+        weights[side, rank] = total.astype(bf16)
+        for copy in shared_out:
+            copy.start()
+
+    def spread_sum():
+        for copy in shared_in:
+            copy.wait_recv()
+        for copy in shared_out:
+            copy.wait_send()
+        doubling.start()
+
     gatherings = [gathering(p) for p in range(n)]
     crossings = [crossing(p) for p in range(n)]
+
+    def cast(j, carry):
+        half[j] = partial[1 - side, j].astype(bf16)
+        return carry
+
+    lax.fori_loop(0, pairs, cast, 0)
     greet(("seq", "head"))
+    halving.start()
     for p in range(min(2, n)):
         gatherings[p].start()
+    first_sum()
     for p in range(n):
         gatherings[p].wait_recv()
         gatherings[p].wait_send()
@@ -305,9 +398,17 @@
         lax.fori_loop(0, requests, add, 0)
         lax.fori_loop(0, slots, place, 0)
         crossings[p].start()
+        if p == (n - 1) // 2:
+            second_sum()
+    spread_sum()
+    halving.wait_send()
+    for copy in sums:
+        copy.wait_send()
     for p in range(n):
         crossings[p].wait_send()
         crossings[p].wait_recv()
+    doubling.wait_send()
+    doubled.wait_recv()
 
 
 def semaphores(n, seq_count, shards):
@@ -336,7 +437,7 @@
         + [pltpu.VMEM((requests, p[1], p[3]), bf16) for p in pieces]
         + semaphores(len(pieces), seq_count, shards),
         compiler_params=pltpu.CompilerParams(
-            collective_id=0, has_side_effects=True, vmem_limit_bytes=40 * 1024 * 1024
+            collective_id=0, has_side_effects=True, vmem_limit_bytes=VMEM_LIMIT
         ),
         cost_estimate=pl.CostEstimate(
             flops=0, bytes_accessed=256 * 1024 * 1024, transcendentals=0
@@ -344,26 +445,33 @@
     )(picked, positions, pool)
 
 
-def give_back(pieces, capacity, seq_count, shards, back, shares):
+def give_back(pieces, capacity, seq_count, shards, back, partial, shares):
     bf16 = jnp.bfloat16
     slots, requests = back.shape[0], shares[0].shape[1]
     hbm = pl.BlockSpec(memory_space=pl.ANY)
+    vmem = pl.BlockSpec(memory_space=pltpu.VMEM)
+    pairs, block = partial.shape[1], partial.shape[2:]
+    dma = pltpu.SemaphoreType.DMA
     return pl.pallas_call(
         functools.partial(return_kernel, pieces, capacity),
-        out_shape=[jax.ShapeDtypeStruct((slots, p[1], p[3]), bf16) for p in pieces],
-        in_specs=[pl.BlockSpec(memory_space=pltpu.SMEM)] + [hbm] * len(pieces),
-        out_specs=[hbm] * len(pieces),
+        out_shape=[jax.ShapeDtypeStruct((slots, p[1], p[3]), bf16) for p in pieces]
+        + [jax.ShapeDtypeStruct(partial.shape, bf16)],
+        in_specs=[pl.BlockSpec(memory_space=pltpu.SMEM), vmem] + [hbm] * len(pieces),
+        out_specs=[hbm] * len(pieces) + [vmem],
         scratch_shapes=[pltpu.VMEM((shards, requests, p[1], p[3]), bf16) for p in pieces]
         + [pltpu.VMEM((requests, p[1], p[3]), bf16) for p in pieces]
         + [pltpu.VMEM((slots, p[1], p[3]), bf16) for p in pieces]
-        + semaphores(len(pieces), seq_count, shards),
+        + semaphores(len(pieces), seq_count, shards)
+        + [pltpu.VMEM((pairs,) + block, bf16)] * 4
+        + [dma((4,))]
+        + [dma((pairs,))] * 4,
         compiler_params=pltpu.CompilerParams(
-            collective_id=1, has_side_effects=True, vmem_limit_bytes=40 * 1024 * 1024
+            collective_id=1, has_side_effects=True, vmem_limit_bytes=VMEM_LIMIT
         ),
         cost_estimate=pl.CostEstimate(
             flops=0, bytes_accessed=256 * 1024 * 1024, transcendentals=0
         ),
-    )(back, *shares)
+    )(back, partial, *shares)
 
 
 def local(queries, pool, w_key, w_value, out_grad, nb_source, nb_slot, nb_count):
@@ -400,14 +508,17 @@
     )
     attended, grad_queries = results[:2]
     shares = results[2 : 2 + len(pieces)]
-    key_partial, value_partial = results[2 + len(pieces) :]
+    partial = results[-1]
+    blocks = partial.reshape(2, seq_count // 2, 2 * enc_width // seq_count, partial.shape[2])
 
     back = positions[None, :] == jnp.arange(slot_span)[:, None]
     back_index = jnp.sum(jnp.where(back, order_ids[None, :], 0), axis=1)
     collect = jnp.logical_and(
         picked_slot[None, :] == jnp.arange(pool_count)[:, None], filled[None, :]
     ).astype(bf16)
-    arrived = give_back(pieces, capacity, seq_count, shards, back_index, shares)
+    *arrived, total = give_back(
+        pieces, capacity, seq_count, shards, back_index, blocks, shares
+    )
     grads = [
         jnp.einsum("pq,qre->pre", collect, part, preferred_element_type=f32) for part in arrived
     ]
@@ -419,7 +530,7 @@
         ],
         axis=1,
     )
-    grad_w_key, grad_w_value = lax.psum((key_partial, value_partial), "seq")
+    grad_w_key, grad_w_value = total.reshape(partial.shape).astype(f32)
     return attended, grad_queries, grad_pool, grad_w_key, grad_w_value
 
 

time: 424 us -> 363 us (0.86)
  waiting for transfers between devices: 40 us -> 0 us
  local copies, waits for them, and re-layouts: 28.8 us -> 10.8 us
  between operations: 14.2 us -> 0.79 us
  Pallas kernels: 333 us -> 338 us
    psum x1 -> x0, waiting for transfers between devices: 40 us -> none  [local(): grad_w_key, grad_w_value = lax.psum((key_partial, value_partial), 'seq')]
    unnamed x35 -> x15, local copies, waits for them, and re-layouts: 27.7 us -> 6.25 us
    pallas_call x1, Pallas kernels: 151 us -> 159 us  [give_back(): pl.pallas_call(functools.partial(return_kernel, pieces, capacity), out_sh...]
    pallas_call x1, Pallas kernels: 66.6 us -> 62.2 us  [attention(): pl.pallas_call(functools.partial(attention_kernel, pieces, shards), grid_...]
  transfers between devices with their start and end apart: 1 -> 0, of which waited for: 1 -> 0; matrix products, arithmetic and copies ran while one was open for 2% -> 0% of each run, Pallas kernels for 36% -> 0%
where the time goes in v3:
time: 363 us; the launch traced here: 356 us
  Pallas kernels  338 us (93%)
  local copies, waits for them, and re-layouts  10.8 us (3%)
  matrix products  4.46 us (1%)
    pallas_call x1, Pallas kernels, give_back(): pl.pallas_call(functools.partial(return_kernel, pieces, capacity), out_sh...  159 us
    pallas_call x1, Pallas kernels, fetch(): pl.pallas_call(functools.partial(fetch_kernel, pieces, capacity), out_sha...  117 us
    pallas_call x1, Pallas kernels, attention(): pl.pallas_call(functools.partial(attention_kernel, pieces, shards), grid_...  62.2 us

profile of v3, /device:TPU:8, one launch (start us, length us, event | category | flops | bytes accessed | tf_op | source)
XLA Modules:
  0.0 355.7 jit_solution(17006226660628781614)
XLA Ops:
  0.6 1.3 dynamic_slice.10.counts
  1.9 0.8 copy.25
  2.7 0.1 reshape.51
  2.8 0.3 convert_reduce_fusion
  3.1 0.0 copy-start.5
  3.1 0.7 select_reduce_fusion.1.back
  3.8 0.2 fusion.9
  4.0 0.1 and.31
  4.1 0.8 copy.26
  4.9 0.1 broadcast_in_dim.36
  5.0 0.2 select_reduce_fusion
  5.2 0.6 reshape.52.picked
  5.8 0.0 copy-done.5
  5.8 116.5 %shard_map.119 = (bf16[4,32,16,512]{3,2,1,0:T(8,128)(2,1)}, bf16[4,32,16,384]{3,2,1,0:T(8,128)(2,1)}, bf16[4,32,16,512]{3,2,1,0:T(8,128)(2,1)}, bf16[4,32,16,384]{3,2,1,0:T(8,128)(2,1)}) custom-call(s32[64]{0:T(128)} %reshape.52.picked, s32[32]{0:T(128)} %copy-done.5, bf16[32,32,896]{2,1,0:T(8,128)(2,1)} %pool.1), custom_call_target="tpu_custom_call" | custom-call | bytes 268435456 | tf_op jit(solution)/shard_map/pallas_call | solution.py:430
  122.4 62.2 %shard_map.120 = (bf16[1024,512]{1,0:T(8,128)(2,1)}, bf16[1024,512]{1,0:T(8,128)(2,1)}, bf16[4,32,16,512]{3,2,1,0:T(8,128)(2,1)}, bf16[4,32,16,384]{3,2,1,0:T(8,...) custom-call(s32[16]{0:T(128)} %dynamic_slice.10.counts, ...), custom_call_target="tpu_custom_call" | custom-call | flops 24159191040 | bytes 33554432 | tf_op jit(solution)/shard_map/pallas_call | solution.py:126
  184.6 0.0 copy-start.4
  184.6 159.2 %shard_map.121 = (bf16[64,16,512]{2,1,0:T(8,128)(2,1)}, bf16[64,16,384]{2,1,0:T(8,128)(2,1)}, bf16[64,16,512]{2,1,0:T(8,128)(2,1)}, bf16[64,16,384]{2,1,0:T(8,128)(2,1)}, bf16[2,4,224,512]{3,2,1,0:T(8,128)(2,1)}) custom-call(s32[64]{0:T(128)} %select_reduce_fusion.1.back, f32[2,4,224,512]{3,2,1,0:T(8,128)} %bitcast.11, ...), custom_call_target="tpu_custom_call" | custom-call | bytes 268435456 | tf_op jit(solution)/shard_map/pallas_call | solution.py:455
  343.8 0.0 copy-start.3
  343.9 0.0 copy-start.2
  343.9 0.0 copy-done.4
  343.9 2.6 fusion.2
  346.5 0.0 copy-done.3
  346.5 0.0 copy-start.1
  346.5 0.3 fusion.6
  346.8 0.0 copy-done.2
  346.8 0.3 fusion.4
  347.1 0.7 copy-done.1
  347.8 1.3 fusion
  349.1 0.3 maximum_maximum_fusion
  349.4 0.0 copy-start
  349.4 4.0 %copy.31 = f32[32,32,896]{2,1,0:T(8,128)} copy(f32[32,32,896]{2,0,1:T(8,128)S(1)} %maximum_maximum_fusion) | data formatting | bytes 7340032
  353.4 2.3 fusion.16
  (4 shorter events, 0.0 us)
Async XLA Ops:
  3.1 2.7 copy-start.5
  184.6 159.3 %copy-start.4 = (s32[64]{0:T(128)S(1)}, s32[64]{0:T(128)}, u32[]{:S(2)}) copy-start(s32[64]{0:T(128)} %reshape.52.picked) | copy-start | bytes 772
  343.8 2.7 copy-start.3
  343.9 3.0 copy-start.2
  346.5 1.2 copy-start.1
  349.4 4.0 %copy-start = (bf16[2,4,224,512]{3,2,1,0:T(8,128)(2,1)S(1)}, bf16[2,4,224,512]{3,2,1,0:T(8,128)(2,1)}, u32[]{:S(2)}) copy-start(bf16[2,4,224,512]{3,2,1,0:T(8,128)(2,1)} %get-tuple-element.36) | copy-start | bytes 5505028

commit v4 on v3

--- a/solution.py
+++ b/solution.py
@@ -15,7 +15,7 @@
 GROUP = 4
 VMEM_LIMIT = 60 * 1024 * 1024
 ROW_TILE = 16
-COL_CUTS = (512, 384)
+COL_CUTS = (128, 256, 256, 256)
 
 
 def chunk_list(rows, width):
@@ -23,10 +23,10 @@
     pieces = []
     for cut in range(rows // step):
         start = 0
-        for cols in COL_CUTS:
+        for cols in COL_CUTS if cut == 0 else COL_CUTS[::-1]:
             pieces.append((cut * step, step, start, cols))
             start += cols
-    assert start == width
+        assert start == width
     return pieces
 
 
@@ -57,33 +57,47 @@
     keys = jnp.dot(x, wk_ref[...], preferred_element_type=f32).astype(bf16)
     values = jnp.dot(x, wv_ref[...], preferred_element_type=f32).astype(bf16)
     factor = 1.0 / math.sqrt(DH)
-    column = lax.broadcasted_iota(jnp.int32, (STRETCH, span), 1)
+    column = lax.broadcasted_iota(jnp.int32, (width // DH * STRETCH, span), 1)
     across = (((1,), (1,)), ((), ()))
     down = (((0,), (0,)), ((), ()))
+    heads = [slice(h * DH, (h + 1) * DH) for h in range(width // DH)]
     for c in range(GROUP):
         used = column < counts[step * GROUP + c] * rows_full
         tokens, rows = slice(c * STRETCH, (c + 1) * STRETCH), slice(c * span, (c + 1) * span)
-        for h in range(width // DH):
-            cols = slice(h * DH, (h + 1) * DH)
-            q, g = q_ref[tokens, cols], g_ref[tokens, cols]
-            key, value = keys[rows, cols], values[rows, cols]
-            scores = lax.dot_general(q, key, across, preferred_element_type=f32) * factor
-            scores = jnp.where(used, scores, -jnp.inf)
-            exps = jnp.exp(scores - jnp.max(scores, axis=1, keepdims=True))
-            probs = exps / jnp.sum(exps, axis=1, keepdims=True)
-            weights = probs.astype(bf16)
-            att_ref[tokens, cols] = jnp.dot(weights, value, preferred_element_type=f32).astype(bf16)
-            dprobs = lax.dot_general(g, value, across, preferred_element_type=f32)
-            row_dot = jnp.sum(probs * dprobs, axis=1, keepdims=True)
-            dscores = (probs * (dprobs - row_dot)).astype(bf16)
+        q = [q_ref[tokens, cols] for cols in heads]
+        g = [g_ref[tokens, cols] for cols in heads]
+        key = [keys[rows, cols] for cols in heads]
+        value = [values[rows, cols] for cols in heads]
+
+        def products(left, right):
+            return jnp.concatenate(
+                [
+                    lax.dot_general(a, b, across, preferred_element_type=f32)
+                    for a, b in zip(left, right)
+                ],
+                axis=0,
+            )
+
+        scores = products(q, key) * factor
+        dprobs = products(g, value)
+        scores = jnp.where(used, scores, -jnp.inf)
+        exps = jnp.exp(scores - jnp.max(scores, axis=1, keepdims=True))
+        probs = exps / jnp.sum(exps, axis=1, keepdims=True)
+        weights = probs.astype(bf16)
+        row_dot = jnp.sum(probs * dprobs, axis=1, keepdims=True)
+        dscores = (probs * (dprobs - row_dot)).astype(bf16)
+        for h, cols in enumerate(heads):
+            part = slice(h * STRETCH, (h + 1) * STRETCH)
+            w, d = weights[part], dscores[part]
+            att_ref[tokens, cols] = jnp.dot(w, value[h], preferred_element_type=f32).astype(bf16)
             gq_ref[tokens, cols] = (
-                jnp.dot(dscores, key, preferred_element_type=f32) * factor
+                jnp.dot(d, key[h], preferred_element_type=f32) * factor
             ).astype(bf16)
             d_ref[rows, cols] = (
-                lax.dot_general(dscores, q, down, preferred_element_type=f32) * factor
+                lax.dot_general(d, q[h], down, preferred_element_type=f32) * factor
             ).astype(bf16)
             d_ref[rows, width + h * DH : width + (h + 1) * DH] = lax.dot_general(
-                weights, g, down, preferred_element_type=f32
+                w, g[h], down, preferred_element_type=f32
             ).astype(bf16)
     both = d_ref[...]
     share = (
@@ -168,6 +182,54 @@
     pl.semaphore_wait(barrier, total)
 
 
+class Relay:
+    def __init__(self, source, target, send, recv, own):
+        size, me = lax.axis_size("head"), lax.axis_index("head")
+        pairs, core, row = size // 2, lax.rem(me, 2), lax.div(me, 2)
+        sibling = 2 * row + 1 - core
+
+        def copy(src, place, sem, device):
+            return pltpu.make_async_remote_copy(
+                src_ref=src,
+                dst_ref=target(place),
+                send_sem=send.at[sem],
+                recv_sem=recv.at[sem],
+                device_id={"head": device},
+                device_id_type=MESH,
+            )
+
+        def at(o, side):
+            return 2 * lax.rem(row + o, pairs) + side
+
+        far = range(1, pairs)
+        self.own = pltpu.make_async_copy(source, target(me), own)
+        self.first = [copy(source, me, 0, sibling)]
+        self.first += [copy(source, me, o, at(o, core)) for o in far]
+        self.arrived = [copy(source, at(pairs - o, core), o, at(o, core)) for o in far]
+        self.second = [
+            copy(target(at(pairs - o, core)), at(pairs - o, core), pairs + o, sibling) for o in far
+        ]
+        self.last = [copy(source, sibling, 0, sibling)]
+        self.last += [copy(source, at(pairs - o, 1 - core), pairs + o, sibling) for o in far]
+
+    def start(self):
+        for copy in self.first:
+            copy.start()
+        self.own.start()
+
+    def forward(self):
+        for here, on in zip(self.arrived, self.second):
+            here.wait_recv()
+            on.start()
+
+    def wait(self):
+        for copy in self.last:
+            copy.wait_recv()
+        for copy in self.first + self.second:
+            copy.wait_send()
+        self.own.wait()
+
+
 class Exchange:
     def __init__(self, axis, source, target, send, recv, own):
         self.size, me, after, before = ring(axis)
@@ -229,9 +291,8 @@
         )
 
     def spreading(p):
-        return Exchange(
-            "head",
-            lambda d: wanted[p],
+        return Relay(
+            wanted[p],
             lambda d: panels[p].at[d],
             head_send.at[p],
             head_recv.at[p],
@@ -259,9 +320,11 @@
 
         lax.fori_loop(0, requests, body, 0)
         spreadings[p].start()
+        if p > 0:
+            spreadings[p - 1].forward()
+    spreadings[n - 1].forward()
     for p in range(n):
-        spreadings[p].wait_send()
-        spreadings[p].wait_recv()
+        spreadings[p].wait()
 
 
 def return_kernel(pieces, capacity, back, partial, *refs):
@@ -375,14 +438,13 @@
     lax.fori_loop(0, pairs, cast, 0)
     greet(("seq", "head"))
     halving.start()
-    for p in range(min(2, n)):
-        gatherings[p].start()
-    first_sum()
+    gatherings[0].start()
     for p in range(n):
         gatherings[p].wait_recv()
         gatherings[p].wait_send()
-        if p + 2 < n:
-            gatherings[p + 2].start()
+        for later in (1, 2) if p == 0 else (p + 2,):
+            if later < n:
+                gatherings[later].start()
 
         def add(j, carry):
             total = got[p][0, j].astype(jnp.float32)
@@ -398,6 +460,8 @@
         lax.fori_loop(0, requests, add, 0)
         lax.fori_loop(0, slots, place, 0)
         crossings[p].start()
+        if p == 0:
+            first_sum()
         if p == (n - 1) // 2:
             second_sum()
     spread_sum()

time: 363 us -> 314 us (0.87); the launches traced: 356 us -> 313 us
  Pallas kernels: 338 us -> 293 us
    pallas_call x1, Pallas kernels: 117 us -> 94.7 us  [fetch(): pl.pallas_call(functools.partial(fetch_kernel, pieces, capacity), out_sha...]
    pallas_call x1, Pallas kernels: 62.2 us -> 44.8 us  [attention(): pl.pallas_call(functools.partial(attention_kernel, pieces, shards), grid_...]
    pallas_call x1, Pallas kernels: 159 us -> 154 us  [give_back(): pl.pallas_call(functools.partial(return_kernel, pieces, capacity), out_sh...]
where the time goes in v4:
time: 314 us; the launch traced here: 313 us
  Pallas kernels  293 us (93%)
  local copies, waits for them, and re-layouts  10.2 us (3%)
  matrix products  7.07 us (2%)
    pallas_call x1, Pallas kernels, give_back(): pl.pallas_call(functools.partial(return_kernel, pieces, capacity), out_sh...  154 us
    pallas_call x1, Pallas kernels, fetch(): pl.pallas_call(functools.partial(fetch_kernel, pieces, capacity), out_sha...  94.7 us
    pallas_call x1, Pallas kernels, attention(): pl.pallas_call(functools.partial(attention_kernel, pieces, shards), grid_...  44.8 us
    dot_general x8, matrix products, local(): jnp.einsum('pq,qre->pre', collect, part, preferred_element_type=f32)  7.07 us

profile of v4, /device:TPU:8, one launch (start us, length us, event | category | flops | bytes accessed | tf_op | source)
XLA Modules:
  0.0 313.1 jit_solution(2111583728386489175)
XLA Ops:
  0.6 1.3 dynamic_slice.10.counts
  2.0 0.8 copy.33
  2.7 0.1 reshape.51
  2.8 0.3 convert_reduce_fusion
  3.2 0.0 copy-start.5
  3.2 0.6 select_reduce_fusion.1.back
  3.8 0.2 fusion.17
  4.0 0.1 and.31
  4.1 0.8 copy.34
  4.9 0.1 broadcast_in_dim.36
  5.0 0.2 select_reduce_fusion
  5.2 0.7 reshape.52.picked
  5.9 0.0 copy-done.5
  5.9 94.7 %shard_map.119 = (bf16[4,32,16,128]{3,2,1,0:T(8,128)(2,1)}, bf16[4,32,16,256]{3,2,1,0:T(8,128)(2,1)}, bf16[4,32,16,256]{3,2,1,0:T(8,128)(2,1)}, bf16[4,32,16,256...) custom-call(s32[64]{0:T(128)} %reshape.52.picked, ...), custom_call_target="tpu_custom_call" | custom-call | bytes 268435456 | tf_op jit(solution)/shard_map/pallas_call | solution.py:494
  100.6 44.8 %shard_map.120 = (bf16[1024,512]{1,0:T(8,128)(2,1)}, bf16[1024,512]{1,0:T(8,128)(2,1)}, bf16[4,32,16,128]{3,2,1,0:T(8,128)(2,1)}, bf16[4,32,16,256]{3,2,1,0:T(8,...) custom-call(s32[16]{0:T(128)} %dynamic_slice.10.counts, ...), custom_call_target="tpu_custom_call" | custom-call | flops 24159191040 | bytes 33554432 | tf_op jit(solution)/shard_map/pallas_call | solution.py:140
  145.4 153.7 %shard_map.121 = (bf16[64,16,128]{2,1,0:T(8,128)(2,1)}, bf16[64,16,256]{2,1,0:T(8,128)(2,1)}, bf16[64,16,256]{2,1,0:T(8,128)(2,1)}, bf16[64,16,256]{2,1,0:T(8,12...) custom-call(s32[64]{0:T(128)} %select_reduce_fusion.1.back, ...), custom_call_target="tpu_custom_call" | custom-call | bytes 268435456 | tf_op jit(solution)/shard_map/pallas_call | solution.py:519
  299.1 0.0 copy-start.3
  299.1 0.0 copy-start.2
  299.1 0.0 copy-start.1
  299.1 0.0 copy-done.4
  299.2 1.2 fusion.14
  300.4 1.1 fusion.12
  301.5 1.3 fusion.10
  302.8 1.3 fusion.8
  304.1 1.3 fusion.6
  305.5 0.3 fusion.4
  305.7 0.3 fusion.2
  306.0 0.3 fusion
  306.3 0.5 maximum_maximum_fusion
  306.8 0.0 copy-start
  306.8 4.0 %copy.43 = f32[32,32,896]{2,1,0:T(8,128)} copy(f32[32,32,896]{2,0,1:T(8,128)S(1)} %maximum_maximum_fusion) | data formatting | bytes 7340032
  310.8 2.3 fusion.28
  (8 shorter events, 0.0 us)
Async XLA Ops:
  3.2 2.7 copy-start.5
  145.4 153.7 %copy-start.4 = (s32[64]{0:T(128)S(1)}, s32[64]{0:T(128)}, u32[]{:S(2)}) copy-start(s32[64]{0:T(128)} %reshape.52.picked) | copy-start | bytes 772
  299.1 6.3 %copy-start.3 = (bf16[64,16,256]{2,1,0:T(8,128)(2,1)S(1)}, bf16[64,16,256]{2,1,0:T(8,128)(2,1)}, u32[]{:S(2)}) copy-start(bf16[64,16,256]{2,1,0:T(8,128)(2,1)} %get-tuple-element.56) | copy-start | bytes 1572868
  299.1 6.6 %copy-start.2 = (bf16[64,16,256]{2,1,0:T(8,128)(2,1)S(1)}, bf16[64,16,256]{2,1,0:T(8,128)(2,1)}, u32[]{:S(2)}) copy-start(bf16[64,16,256]{2,1,0:T(8,128)(2,1)} %get-tuple-element.57) | copy-start | bytes 1572868
  299.1 6.9 %copy-start.1 = (bf16[64,16,256]{2,1,0:T(8,128)(2,1)S(1)}, bf16[64,16,256]{2,1,0:T(8,128)(2,1)}, u32[]{:S(2)}) copy-start(bf16[64,16,256]{2,1,0:T(8,128)(2,1)} %get-tuple-element.58) | copy-start | bytes 1572868
  306.8 4.0 %copy-start = (bf16[2,4,224,512]{3,2,1,0:T(8,128)(2,1)S(1)}, bf16[2,4,224,512]{3,2,1,0:T(8,128)(2,1)}, u32[]{:S(2)}) copy-start(bf16[2,4,224,512]{3,2,1,0:T(8,128)(2,1)} %get-tuple-element.60) | copy-start | bytes 5505028

commit v5 on v4

--- a/solution.py
+++ b/solution.py
@@ -333,7 +333,7 @@
     weights = refs[2 * n]
     got, summed, returning = (refs[2 * n + 1 + i * n : 2 * n + 1 + (i + 1) * n] for i in range(3))
     seq_send, seq_recv, seq_own, head_send, head_recv, head_own = refs[5 * n + 1 : 5 * n + 7]
-    half, half_in, mine, mine_in, pair_sem, sum_send, sum_recv, all_send, all_recv = refs[
+    half, half_in, mine, running, mine_in, pair_sem, sum_send, sum_recv, all_send, all_recv = refs[
         5 * n + 7 :
     ]
     f32, bf16 = jnp.float32, jnp.bfloat16
@@ -374,59 +374,80 @@
             device_id_type=MESH,
         )
 
-    def at(o):
-        return lax.rem(rank + o, pairs)
-
-    others = range(1, pairs)
     partner = 2 * rank + 1 - side
     halving = to_seq(half, half_in, pair_sem.at[0], pair_sem.at[1], partner)
     doubling = to_seq(weights.at[side], weights.at[side], pair_sem.at[2], pair_sem.at[3], partner)
     doubled = to_seq(
         weights.at[side], weights.at[1 - side], pair_sem.at[2], pair_sem.at[3], partner
     )
-    sums = [
-        to_seq(mine.at[at(o)], mine_in.at[o], sum_send.at[o], sum_recv.at[o], 2 * at(o) + side)
-        for o in others
-    ]
-
-    def sharing(o, place):
-        return to_seq(
-            weights.at[side, rank],
-            weights.at[side, place],
-            all_send.at[o],
-            all_recv.at[o],
-            2 * at(o) + side,
+    levels, bit, taken = [], 1, 0
+    while bit < pairs:
+        near, away = lax.rem(rank, 2 * bit), lax.rem(rank + bit, 2 * bit)
+        device = 2 * (rank - near + away) + side
+        steps = [2 * bit * m for m in range(pairs // (2 * bit))]
+        kept, given = [near + m for m in steps], [away + m for m in steps]
+        box = mine_in.at[len(levels)]
+
+        def summing(places):
+            return [
+                to_seq(mine.at[j], box.at[j], sum_send.at[k], sum_recv.at[k], device)
+                for k, j in enumerate(places, taken)
+            ]
+
+        def sharing(places):
+            return [
+                to_seq(
+                    weights.at[side, j], weights.at[side, j], all_send.at[k], all_recv.at[k], device
+                )
+                for k, j in enumerate(places, taken)
+            ]
+
+        levels.append(
+            (kept, box, summing(given), summing(kept), sharing(kept), sharing(given))
         )
-
-    shared_out = [sharing(o, rank) for o in others]
-    shared_in = [sharing(o, at(pairs - o)) for o in others]
+        taken += len(steps)
+        bit *= 2
 
     def first_sum():
         halving.wait_recv()
 
         def body(j, carry):
-            mine[j] = (partial[side, j] + half_in[j].astype(f32)).astype(bf16)
+            total = partial[side, j] + half_in[j].astype(f32)
+            running[j] = total
+            mine[j] = total.astype(bf16)
             return carry
 
         lax.fori_loop(0, pairs, body, 0)
-        for copy in sums:
+        for copy in levels[0][2]:
             copy.start()
 
-    def second_sum():
-        total = partial[side, rank] + half_in[rank].astype(f32)
-        for o, copy in zip(others, sums):
+    def level_sum(i):
+        kept, box, _, inward = levels[i][:4]
+        for j, copy in zip(kept, inward):
             copy.wait_recv()
-            total += mine_in[o].astype(f32)
-        weights[side, rank] = total.astype(bf16)
-        for copy in shared_out:
-            copy.start()
-
-    def spread_sum():
-        for copy in shared_in:
+            total = running[j] + box[j].astype(f32)
+            running[j] = total
+            mine[j] = total.astype(bf16)
+        if i + 1 < len(levels):
+            for copy in levels[i + 1][2]:
+                copy.start()
+        else:
+            weights[side, rank] = mine[rank]
+            for copy in levels[i][4]:
+                copy.start()
+
+    def level_share(i):
+        for copy in levels[i][5]:
             copy.wait_recv()
-        for copy in shared_out:
-            copy.wait_send()
-        doubling.start()
+        if i > 0:
+            for copy in levels[i - 1][4]:
+                copy.start()
+        else:
+            doubling.start()
+
+    actions = [first_sum]
+    actions += [functools.partial(level_sum, i) for i in range(len(levels))]
+    actions += [functools.partial(level_share, i) for i in reversed(range(len(levels)))]
 
     gatherings = [gathering(p) for p in range(n)]
     crossings = [crossing(p) for p in range(n)]
@@ -460,14 +481,14 @@
         lax.fori_loop(0, requests, add, 0)
         lax.fori_loop(0, slots, place, 0)
         crossings[p].start()
-        if p == 0:
-            first_sum()
-        if p == (n - 1) // 2:
-            second_sum()
-    spread_sum()
+        if p < len(actions):
+            actions[p]()
+    for action in actions[n:]:
+        action()
     halving.wait_send()
-    for copy in sums:
-        copy.wait_send()
+    for level in levels:
+        for copy in level[2] + level[4]:
+            copy.wait_send()
     for p in range(n):
         crossings[p].wait_send()
         crossings[p].wait_recv()
@@ -526,7 +547,9 @@
         + [pltpu.VMEM((requests, p[1], p[3]), bf16) for p in pieces]
         + [pltpu.VMEM((slots, p[1], p[3]), bf16) for p in pieces]
         + semaphores(len(pieces), seq_count, shards)
-        + [pltpu.VMEM((pairs,) + block, bf16)] * 4
+        + [pltpu.VMEM((pairs,) + block, bf16)] * 3
+        + [pltpu.VMEM((pairs,) + block, jnp.float32)]
+        + [pltpu.VMEM((pairs.bit_length() - 1, pairs) + block, bf16)]
         + [dma((4,))]
         + [dma((pairs,))] * 4,
         compiler_params=pltpu.CompilerParams(

time: 314 us -> 295 us (0.939)
  Pallas kernels: 293 us -> 275 us
    pallas_call x1, Pallas kernels: 154 us -> 135 us  [give_back(): pl.pallas_call(functools.partial(return_kernel, pieces, capacity), out_sh...]
where the time goes in v5:
time: 295 us
  Pallas kernels  275 us (93%)
  local copies, waits for them, and re-layouts  10.2 us (3%)
  matrix products  7.07 us (2%)
    pallas_call x1, Pallas kernels, give_back(): pl.pallas_call(functools.partial(return_kernel, pieces, capacity), out_sh...  135 us
    pallas_call x1, Pallas kernels, fetch(): pl.pallas_call(functools.partial(fetch_kernel, pieces, capacity), out_sha...  94.7 us
    pallas_call x1, Pallas kernels, attention(): pl.pallas_call(functools.partial(attention_kernel, pieces, shards), grid_...  44.8 us
    dot_general x8, matrix products, local(): jnp.einsum('pq,qre->pre', collect, part, preferred_element_type=f32)  7.07 us

profile of v5, /device:TPU:8, one launch (start us, length us, event | category | flops | bytes accessed | tf_op | source)
XLA Modules:
  0.0 294.5 jit_solution(13560449632967507667)
XLA Ops:
  0.6 1.3 dynamic_slice.10.counts
  2.0 0.8 copy.33
  2.7 0.1 reshape.51
  2.8 0.3 convert_reduce_fusion
  3.2 0.0 copy-start.5
  3.2 0.6 select_reduce_fusion.1.back
  3.8 0.2 fusion.17
  4.0 0.1 and.31
  4.1 0.8 copy.34
  4.9 0.1 broadcast_in_dim.36
  5.0 0.2 select_reduce_fusion
  5.2 0.7 reshape.52.picked
  5.9 0.0 copy-done.5
  5.9 94.7 %shard_map.119 = (bf16[4,32,16,128]{3,2,1,0:T(8,128)(2,1)}, bf16[4,32,16,256]{3,2,1,0:T(8,128)(2,1)}, bf16[4,32,16,256]{3,2,1,0:T(8,128)(2,1)}, bf16[4,32,16,256...) custom-call(s32[64]{0:T(128)} %reshape.52.picked, ...), custom_call_target="tpu_custom_call" | custom-call | bytes 268435456 | tf_op jit(solution)/shard_map/pallas_call | solution.py:515
  100.6 44.8 %shard_map.120 = (bf16[1024,512]{1,0:T(8,128)(2,1)}, bf16[1024,512]{1,0:T(8,128)(2,1)}, bf16[4,32,16,128]{3,2,1,0:T(8,128)(2,1)}, bf16[4,32,16,256]{3,2,1,0:T(8,...) custom-call(s32[16]{0:T(128)} %dynamic_slice.10.counts, ...), custom_call_target="tpu_custom_call" | custom-call | flops 24159191040 | bytes 33554432 | tf_op jit(solution)/shard_map/pallas_call | solution.py:140
  145.4 0.0 copy-start.4
  145.4 135.3 %shard_map.121 = (bf16[64,16,128]{2,1,0:T(8,128)(2,1)}, bf16[64,16,256]{2,1,0:T(8,128)(2,1)}, bf16[64,16,256]{2,1,0:T(8,128)(2,1)}, bf16[64,16,256]{2,1,0:T(8,12...) custom-call(s32[64]{0:T(128)} %select_reduce_fusion.1.back, ...), custom_call_target="tpu_custom_call" | custom-call | bytes 268435456 | tf_op jit(solution)/shard_map/pallas_call | solution.py:540
  280.7 0.0 copy-start.3
  280.7 1.2 fusion.14
  282.0 1.1 fusion.12
  283.1 1.3 fusion.10
  284.4 1.3 fusion.8
  285.7 1.3 fusion.6
  287.0 0.0 copy-done.3
  287.0 0.3 fusion.4
  287.3 0.0 copy-done.2
  287.3 0.3 fusion.2
  287.6 0.3 fusion
  287.9 0.4 maximum_maximum_fusion
  288.2 0.0 copy-start
  288.2 4.0 %copy.43 = f32[32,32,896]{2,1,0:T(8,128)} copy(f32[32,32,896]{2,0,1:T(8,128)S(1)} %maximum_maximum_fusion) | data formatting | bytes 7340032
  292.2 2.3 fusion.28
  (8 shorter events, 0.0 us)
Async XLA Ops:
  3.2 2.7 copy-start.5
  145.4 135.3 %copy-start.4 = (s32[64]{0:T(128)S(1)}, s32[64]{0:T(128)}, u32[]{:S(2)}) copy-start(s32[64]{0:T(128)} %reshape.52.picked) | copy-start | bytes 772
  280.7 6.3 %copy-start.3 = (bf16[64,16,256]{2,1,0:T(8,128)(2,1)S(1)}, bf16[64,16,256]{2,1,0:T(8,128)(2,1)}, u32[]{:S(2)}) copy-start(bf16[64,16,256]{2,1,0:T(8,128)(2,1)} %get-tuple-element.56) | copy-start | bytes 1572868
  280.7 6.6 %copy-start.2 = (bf16[64,16,256]{2,1,0:T(8,128)(2,1)S(1)}, bf16[64,16,256]{2,1,0:T(8,128)(2,1)}, u32[]{:S(2)}) copy-start(bf16[64,16,256]{2,1,0:T(8,128)(2,1)} %get-tuple-element.57) | copy-start | bytes 1572868
  280.7 6.9 %copy-start.1 = (bf16[64,16,256]{2,1,0:T(8,128)(2,1)S(1)}, bf16[64,16,256]{2,1,0:T(8,128)(2,1)}, u32[]{:S(2)}) copy-start(bf16[64,16,256]{2,1,0:T(8,128)(2,1)} %get-tuple-element.58) | copy-start | bytes 1572868
  288.2 4.0 %copy-start = (bf16[2,4,224,512]{3,2,1,0:T(8,128)(2,1)S(1)}, bf16[2,4,224,512]{3,2,1,0:T(8,128)(2,1)}, u32[]{:S(2)}) copy-start(bf16[2,4,224,512]{3,2,1,0:T(8,128)(2,1)} %get-tuple-element.60) | copy-start | bytes 5505028
